TPU v7x, 128 devices: a whole 4x4x4 slice. The times are simulated.
128 devices in a mesh: row: 16 (over x, z_hi, core), col: 8 (over y, z_lo).
Axes of the slice: x: 4, y: 4, z: 4 (z_hi: 2, z_lo: 2; z = z_hi * 2 + z_lo), core: 2. Of those that a mesh axis runs over, the one named last changes fastest.
Arguments:
- nodes: bfloat16 [131072, 256], P(('row', 'col')), may hold values from -6 to 6
- tiles: bfloat16 [1024, 8, 4, 128, 128], P('row', 'col'), may hold values from -0.12988281 to 0.12988281
- tile_col: int32 [1024, 8, 4], P('row', 'col'), may hold values from 0 to 127, as said below
- tile_count: int32 [1024, 8], P('row', 'col'), may hold values from 0 to 4, as said below
- w_in: bfloat16 [512, 256], replicated, may hold values from -0.25 to 0.25
- bias_in: float32 [256], replicated, may hold values from -3 to 3
- w_out: bfloat16 [256, 256], replicated, may hold values from -0.375 to 0.375
- ln_gain: float32 [256], replicated, may hold values from 0.1 to 1.9
- ln_shift: float32 [256], replicated, may hold values from -3 to 3
- cotangent: bfloat16 [131072, 256], P(('row', 'col')), may hold values from -6 to 6
Outputs:
- updated: bfloat16 [131072, 256], P(('row', 'col'))
- grad_nodes: bfloat16 [131072, 256], P(('row', 'col'))
- grad_tiles: bfloat16 [1024, 8, 4, 128, 128], P('row', 'col')
- grad_w_in: float32 [512, 256], replicated
- grad_w_out: float32 [256, 256], replicated
- grad_vectors: float32 [3, 256], replicated
Inputs may be any that keep to these rules, and one draw needn't show every extreme that they name: `tile_col`: index within the column group; slots at or past the block row's tile_count are ignored. `tile_count`: loads differ between devices; 4 is reached in every draw.
All inputs are finite; a program needn't handle non-finite values.
Results may differ from a plain program's by a relative error of at most 0.02.
Values may be sent and summed in bfloat16 or wider, within the bound.
A program may use at most 256 MiB of HBM per device.

v0:
```python
import jax
import jax.numpy as jnp
from jax import lax
from jax.sharding import PartitionSpec as P


def pick_blocks(gathered, cols, block, width):
    blocks = gathered.reshape(-1, block, width)
    return blocks[cols]


def body(nodes, tiles, tile_col, tile_count, w_in, bias_in, w_out, ln_gain, ln_shift, cotangent):
    rows, width = nodes.shape
    row_blocks, slots, block = (tiles.shape[0], tiles.shape[2], tiles.shape[3])
    tile_local = tiles[:, 0]
    cols = tile_col[:, 0]
    count = tile_count[:, 0]
    live = lax.broadcasted_iota(jnp.int32, (row_blocks, slots), 1) < count[:, None]
    live_tiles = jnp.where(live[:, :, None, None], tile_local, jnp.zeros((), tile_local.dtype))
    gathered = lax.all_gather(nodes, "row", axis=0, tiled=True)
    picked = pick_blocks(gathered, cols, block, width)
    partial_value = jnp.einsum(
        "rkij,rkjd->rid", live_tiles, picked, preferred_element_type=jnp.float32
    )
    summed = lax.psum_scatter(
        partial_value.reshape(row_blocks * block, width).astype(jnp.bfloat16),
        "col",
        scatter_dimension=0,
        tiled=True,
    )
    pre = (
        jnp.dot(nodes, w_in[:width], preferred_element_type=jnp.float32)
        + jnp.dot(summed, w_in[width:], preferred_element_type=jnp.float32)
        + bias_in
    )
    sig = jax.nn.sigmoid(pre)
    act = (pre * sig).astype(jnp.bfloat16)
    proj = jnp.dot(act, w_out, preferred_element_type=jnp.float32)
    mean = jnp.mean(proj, axis=-1, keepdims=True)
    var = jnp.mean((proj - mean) ** 2, axis=-1, keepdims=True)
    rstd = 1.0 / jnp.sqrt(var + 1e-05)
    normed = (proj - mean) * rstd
    updated = (nodes.astype(jnp.float32) + normed * ln_gain + ln_shift).astype(jnp.bfloat16)
    grad_out = cotangent.astype(jnp.float32)
    gscaled = grad_out * ln_gain
    gproj = (
        (
            gscaled
            - jnp.mean(gscaled, axis=-1, keepdims=True)
            - normed * jnp.mean(gscaled * normed, axis=-1, keepdims=True)
        )
        * rstd
    ).astype(jnp.bfloat16)
    gact = jnp.dot(gproj, w_out.T, preferred_element_type=jnp.float32)
    gpre = gact * sig * (1.0 + pre * (1.0 - sig))
    gpre_b = gpre.astype(jnp.bfloat16)
    gmsg = jnp.dot(gpre_b, w_in[width:].T, preferred_element_type=jnp.float32).astype(jnp.bfloat16)
    direct = grad_out + jnp.dot(gpre_b, w_in[:width].T, preferred_element_type=jnp.float32)
    grad_rows = lax.all_gather(gmsg, "col", axis=0, tiled=True).reshape(row_blocks, block, width)
    back = jnp.einsum("rkij,rid->rkjd", live_tiles, grad_rows, preferred_element_type=jnp.float32)
    col_blocks = gathered.shape[0] // block
    flat_back = back.reshape(row_blocks * slots, block * width)
    flat_cols = cols.reshape(-1)
    column_terms = jax.ops.segment_sum(flat_back, flat_cols, num_segments=col_blocks)
    column_terms = column_terms.astype(jnp.bfloat16)
    agg = lax.psum_scatter(
        column_terms.reshape(col_blocks * block, width), "row", scatter_dimension=0, tiled=True
    ).astype(jnp.float32)
    grad_nodes = (direct + agg).astype(jnp.bfloat16)
    tile_grads = jnp.einsum("rid,rkjd->rkij", grad_rows, picked, preferred_element_type=jnp.float32)
    tile_grads = jnp.where(
        live[:, :, None, None], tile_grads * jnp.float32(width) ** (-0.5), jnp.float32(0.0)
    )
    grad_tiles = tile_grads.astype(jnp.bfloat16)[:, None]
    total_nodes = rows * lax.axis_size("row") * lax.axis_size("col")
    factor = jnp.float32(total_nodes) ** (-0.5)
    local_in = jnp.concatenate(
        [
            jnp.dot(nodes.T, gpre_b, preferred_element_type=jnp.float32),
            jnp.dot(summed.T, gpre_b, preferred_element_type=jnp.float32),
        ],
        axis=0,
    )
    local_out = jnp.dot(act.T, gproj, preferred_element_type=jnp.float32)
    local_vectors = jnp.stack(
        [jnp.sum(gpre, axis=0), jnp.sum(grad_out * normed, axis=0), jnp.sum(grad_out, axis=0)]
    )
    sum_in, sum_out, sum_vectors = lax.psum((local_in, local_out, local_vectors), ("row", "col"))
    return (
        updated,
        grad_nodes,
        grad_tiles,
        sum_in * factor,
        sum_out * factor,
        sum_vectors * factor,
    )


def solution(mesh):
    placed = (
        P(("row", "col"), None),
        P("row", "col", None, None, None),
        P("row", "col", None),
        P("row", "col"),
        P(),
        P(),
        P(),
        P(),
        P(),
        P(("row", "col"), None),
    )
    return jax.shard_map(
        body,
        mesh=mesh,
        in_specs=placed,
        out_specs=(
            P(("row", "col"), None),
            P(("row", "col"), None),
            P("row", "col", None, None, None),
            P(),
            P(),
            P(),
        ),
        check_vma=False,
    )
```

profile of v0, /device:TPU:1, one launch (start us, length us, event | category | flops | bytes accessed | tf_op | source)
XLA Modules:
  0.0 568.9 jit_solution(246042530562776285)
XLA Ops:
  7.2 0.0 copy-start
  7.2 0.0 all-gather.3.cloned.1.call-start
  7.2 0.7 all-gather.3.cloned.1.call-update
  7.9 0.0 reduce-scatter.3.cloned.1.call-start
  8.0 0.7 compare_select_fusion
  8.7 0.1 copy.24
  8.7 0.1 reshape.104
  8.9 0.7 iota_compare_fusion
  9.6 77.2 %all-gather.3.cloned.1.call-done = bf16[16384,256]{1,0:T(8,128)(2,1)} async-done(((bf16[1024,256]{1,0:T(8,128)(2,1)}), bf16[16384,256]{1,0:T(8,128)(2,1)}) %all-gather.3.cloned.1.call-update) | async-done | bytes 8388624 | tf_op jit(solution)/shard_map/all_gather | solution.py:20
  86.8 13.2 %gather_fusion = bf16[256,128,256]{2,1,0:T(8,128)(2,1)} fusion(bf16[128,128,256]{2,1,0:T(8,128)(2,1)} %bitcast.55, s32[1024]{0:T(1024)S(1)} %pad_clamp_fusion), kind=kCustom, calls=%fused_computation | custom fusion | bytes 33555456 | tf_op jit(solution)/shard_map/gather | solution.py:9
  100.0 0.0 copy-start.2
  100.0 12.7 %bitcast_convert_fusion = bf16[64,128,256]{2,1,0:T(8,128)(2,1)} fusion(bf16[64,4,128,256]{3,2,1,0:T(8,128)(2,1)} %bitcast.57, bf16[64,1,4,128,128]{4,3,2,1,0:T(8,128)(2,1)} %param.11, pred[64,4]{1,0:T(8,128)(4,1)S(1)} %iota_compare_fusion), kind=kOutput, calls=%fused_computation.4 | convolution fusion | flops 2153775104 | bytes 29360384 | tf_op jit(solution)/shard_map/rkij,rkjd->rid/dot_general | solution.py:22
  112.7 0.0 reduce-scatter.3.cloned.1.call-update
  112.8 0.0 all-gather.5.cloned.1.call-start
  112.8 0.0 copy-done.2
  112.8 0.2 copy.23
  113.0 0.0 copy-done.4
  113.1 0.2 copy.25
  113.3 0.0 copy-done.3
  113.3 0.3 fusion.22
  113.6 86.9 %reduce-scatter.3.cloned.1.call-done = bf16[1024,256]{1,0:T(8,128)(2,1)} async-done(((bf16[8192,256]{1,0:T(8,128)(2,1)}), bf16[1024,256]{1,0:T(8,128)(2,1)}) %reduce-scatter.3.cloned.1.call-update) | async-done | bytes 524304 | tf_op jit(solution)/shard_map/reduce_scatter | solution.py:25
  200.5 0.0 copy-done.9
  200.5 1.5 multiply_convert_fusion
  202.0 0.0 copy-start.5
  202.1 0.0 copy-done
  202.1 0.4 fusion.27
  202.4 0.1 multiply_reduce_fusion
  202.6 0.0 copy-done.6
  202.6 1.0 fusion.18
  203.6 1.2 fusion.16
  204.9 0.6 fusion.26
  205.4 1.1 convolution_convert_fusion
  206.5 0.0 all-gather.5.cloned.1.call-update
  206.6 0.0 all-reduce.3.cloned.1.call-start
  206.6 0.0 copy-done.5
  206.6 0.1 copy.27
  206.7 0.1 reshape.112
  206.8 0.4 convolution_bitcast_fusion
  207.2 1.4 fusion.28
  208.6 0.8 pad_maximum_fusion
  209.4 1.1 fusion.29
  210.4 0.0 all-reduce.3.cloned.1.call-update
  210.5 0.3 reduce-scatter.5.cloned.1.call-start
  210.8 86.6 %all-gather.5.cloned.1.call-done = bf16[8192,256]{1,0:T(8,128)(2,1)} async-done(((bf16[1024,256]{1,0:T(8,128)(2,1)}), bf16[8192,256]{1,0:T(8,128)(2,1)}) %all-gather.5.cloned.1.call-update) | async-done | bytes 4194320 | tf_op jit(solution)/shard_map/all_gather | solution.py:59
  297.4 17.7 %fusion.3 = f32[64,4,128,256]{3,2,1,0:T(8,128)} fusion(bf16[64,128,256,1]{2,1,3,0:T(8,128)(2,1)} %bitcast.59, bf16[64,1,4,128,128]{4,3,2,1,0:T(8,128)(2,1)} %param.11, pred[64,4]{1,0:T(8,128)(4,1)S(1)} %iota_compare_fusion), kind=kOutput, calls=%fused_computation.8 | convolution fusion | flops 2151677952 | bytes 46137600 | tf_op jit(solution)/shard_map/rkij,rid->rkjd/dot_general | solution.py:60
  315.1 31.8 %copy.37 = f32[32,8,128,256]{3,1,2,0:T(8,128)} copy(f32[32,8,128,256]{3,2,1,0:T(8,128)} %bitcast.54) | data formatting | bytes 67108864
  346.9 73.3 %scatter_custom_fusion = f32[128,32768]{1,0:T(8,128)} fusion(s32[256]{0:T(256)S(1)} %reshape.112, f32[256,32768]{1,0:T(8,128)} %bitcast.56, f32[]{:T(128)} %constant.7.clone.1), kind=kCustom, calls=%fused_computation.6 | custom fusion | flops 8388608 | bytes 16777728 | tf_op jit(solution)/shard_map/scatter-add | solution.py:64
  420.2 8.9 %convert_element_type.51 = bf16[128,32768]{1,0:T(8,128)(2,1)} convert(f32[128,32768]{1,0:T(8,128)} %scatter_custom_fusion) | non-fusion elementwise | flops 4194304 | bytes 25165824 | tf_op jit(solution)/shard_map/convert_element_type | solution.py:65
  429.1 13.5 %reshape.101 = bf16[16384,256]{1,0:T(8,128)(2,1)} reshape(bf16[128,32768]{1,0:T(8,128)(2,1)} %convert_element_type.51) | data formatting | bytes 16777216 | tf_op jit(solution)/shard_map/reshape | solution.py:67
  442.6 11.9 %copy.29 = bf16[16384,256]{0,1:T(8,128)(2,1)} copy(bf16[16384,256]{1,0:T(8,128)(2,1)} %reshape.101) | data formatting | bytes 16777216 | tf_op jit(solution)/shard_map/reshape | solution.py:67
  454.5 0.0 reduce-scatter.5.cloned.1.call-update
  454.5 1.0 copy.30
  455.5 0.0 copy-done.7
  455.5 0.0 copy-done.8
  455.5 69.0 %psum.23 = f32[3,256]{1,0:T(4,128)S(1)} all-reduce(f32[3,256]{1,0:T(4,128)S(1)} %pad_maximum_fusion.1), channel_id=1, replica_groups=mesh['row'=16,'col'=8] {'row','col'}, use_global_device_ids=true, to_apply=%region_12.13 | all-reduce | flops 768 | bytes 6144 | tf_op jit(solution)/shard_map/psum | solution.py:88
  524.6 0.6 broadcast_multiply_fusion.2
  525.2 1.7 broadcast_multiply_fusion.1
  526.8 1.9 broadcast_multiply_fusion
  528.7 11.4 %fusion = bf16[64,1,4,128,128]{3,4,2,0,1:T(8,128)(2,1)} fusion(pred[64,4]{1,0:T(8,128)(4,1)S(1)} %iota_compare_fusion, bf16[64,4,128,256]{3,2,1,0:T(8,128)(2,1)} %bitcast.58, bf16[64,128,256,1]{2,1,3,0:T(8,128)(2,1)} %bitcast.60), kind=kOutput, calls=%fused_computation.3 | convolution fusion | flops 2160066560 | bytes 29360384 | tf_op jit(solution)/shard_map/rid,rkjd->rkij/dot_general | solution.py:70
  540.1 12.0 %copy.32 = bf16[64,1,4,128,128]{4,3,2,1,0:T(8,128)(2,1)} copy(bf16[64,1,4,128,128]{3,4,2,0,1:T(8,128)(2,1)} %fusion) | data formatting | bytes 16777216
  552.1 7.5 %reduce-scatter.5.cloned.1.call-done = bf16[1024,256]{0,1:T(8,128)(2,1)} async-done(((bf16[16384,256]{0,1:T(8,128)(2,1)}), bf16[1024,256]{0,1:T(8,128)(2,1)}) %reduce-scatter.5.cloned.1.call-update) | async-done | bytes 524304 | tf_op jit(solution)/shard_map/reduce_scatter | solution.py:66
  559.5 1.4 fusion.13
  560.9 1.0 copy.31
  561.9 0.0 copy-done.1
  (13 shorter events, 0.0 us)
Async XLA Ops:
  7.2 194.9 %copy-start = (bf16[256,256]{1,0:T(8,128)(2,1)S(1)}, bf16[256,256]{1,0:T(8,128)(2,1)}, u32[]{:S(2)}) copy-start(bf16[256,256]{1,0:T(8,128)(2,1)} %param.16) | copy-start | bytes 393220
  7.2 79.6 %all-gather.3.cloned.1.call-start = ((), (), s32[]{:S(2)}) async-start(), calls=%async_computation.2 | async-start | bytes 8912896 | tf_op jit(solution)/shard_map/all_gather | solution.py:20
  7.9 192.6 %reduce-scatter.3.cloned.1.call-start = ((), (), s32[]{:S(2)}) async-start(), calls=%async_computation.3 | async-start | bytes 4718592 | tf_op jit(solution)/shard_map/reduce_scatter | solution.py:25
  100.0 12.8 %copy-start.2 = (bf16[1024,256]{1,0:T(8,128)(2,1)S(1)}, bf16[1024,256]{1,0:T(8,128)(2,1)}, u32[]{:S(2)}) copy-start(bf16[1024,256]{1,0:T(8,128)(2,1)} %param.10) | copy-start | bytes 1572868
  100.0 13.0 %copy-start.4 = (bf16[1024,256]{1,0:T(8,128)(2,1)S(1)}, bf16[1024,256]{1,0:T(8,128)(2,1)}, u32[]{:S(2)}) copy-start(bf16[1024,256]{1,0:T(8,128)(2,1)} %param.19) | copy-start | bytes 1572868
  100.0 13.2 %copy-start.3 = (bf16[512,256]{1,0:T(8,128)(2,1)S(1)}, bf16[512,256]{1,0:T(8,128)(2,1)}, u32[]{:S(2)}) copy-start(bf16[512,256]{1,0:T(8,128)(2,1)} %param.14) | copy-start | bytes 786436
  100.0 100.5 %copy-start.9 = (f32[256]{0:T(256)S(1)}, f32[256]{0:T(256)}, u32[]{:S(2)}) copy-start(f32[256]{0:T(256)} %param.15) | copy-start | bytes 3076
  112.7 89.8 %copy-start.6 = (f32[256]{0:T(256)S(1)}, f32[256]{0:T(256)}, u32[]{:S(2)}) copy-start(f32[256]{0:T(256)} %param.17) | copy-start | bytes 3076
  112.8 184.6 %all-gather.5.cloned.1.call-start = ((), (), s32[]{:S(2)}) async-start(), calls=%async_computation.4 | async-start | bytes 4718592 | tf_op jit(solution)/shard_map/all_gather | solution.py:59
  202.0 4.6 copy-start.5
  206.6 318.6 %all-reduce.3.cloned.1.call-start = ((), (), s32[]{:S(2)}) async-start(), calls=%async_computation.6 | async-start | bytes 1572864 | tf_op jit(solution)/shard_map/psum | solution.py:88
  210.5 349.1 %reduce-scatter.5.cloned.1.call-start = ((), (), s32[]{:S(2)}) async-start(), calls=%async_computation.5 | async-start | bytes 8912896 | tf_op jit(solution)/shard_map/reduce_scatter | solution.py:66
  454.5 1.0 copy-start.7
  454.5 1.0 copy-start.8
  528.7 33.2 %copy-start.1 = (bf16[256,256]{1,0:T(8,128)(2,1)S(1)}, bf16[256,256]{1,0:T(8,128)(2,1)}, u32[]{:S(2)}) copy-start(bf16[256,256]{1,0:T(8,128)(2,1)} %param.16) | copy-start | bytes 393220
Sparse Core Ops, SparseCore 0:
  10.4 76.3 all-gather.2
  112.9 87.5 reduce-scatter.2
  206.7 90.6 all-gather.4
  302.6 149.0 all-reduce.2
  455.9 103.6 reduce-scatter.4
where the time goes:
time: 577 us; the launch traced here: 569 us
  waiting for transfers between devices  259 us (45%)
  other arithmetic  91 us (16%)
  local copies, waits for them, and re-layouts  85.2 us (15%)
  blocking collectives  69 us (12%)
  matrix products  49.8 us (9%)
  between operations  14.3 us (2%)
    reduce_scatter x1, waiting for transfers between devices, body(): lax.psum_scatter(partial_value.reshape(row_blocks * block, width).astype(...  86.9 us
    all_gather x1, waiting for transfers between devices, body(): lax.all_gather(gmsg, 'col', axis=0, tiled=True)  86.6 us
    all_gather x1, waiting for transfers between devices, body(): gathered = lax.all_gather(nodes, 'row', axis=0, tiled=True)  77.2 us
    scatter-add x1, other arithmetic, body(): jax.ops.segment_sum(flat_back, flat_cols, num_segments=col_blocks)  73.3 us
    psum x1, blocking collectives, body(): lax.psum((local_in, local_out, local_vectors), ('row', 'col'))  69 us
    unnamed x27, local copies, waits for them, and re-layouts  46.3 us
    reshape x2, local copies, waits for them, and re-layouts, body(): column_terms.reshape(col_blocks * block, width)  25.4 us
    dot_general x1, matrix products, body(): jnp.einsum('rkij,rid->rkjd', live_tiles, grad_rows, preferred_element_typ...  17.7 us
  transfers between devices with their start and end apart: 5, of which 4 were waited for; matrix products, arithmetic and copies ran while one was open for 34% of the time, Pallas kernels for 0%

commit v1 on v0

v1 whole, which is shorter than its diff:
```python
import functools

import jax
import jax.numpy as jnp
from jax import lax
from jax.experimental import pallas as pl
from jax.experimental.pallas import tpu as pltpu
from jax.sharding import PartitionSpec as P

F32, BF16 = jnp.float32, jnp.bfloat16
MIB = 1024 * 1024
VMEM_LIMIT = 56 * MIB
EPS = 1e-05


class Place:
    def __init__(self):
        self.row = lax.axis_index("row")
        self.col = lax.axis_index("col")
        self.x = lax.div(self.row, 4)
        self.zh = lax.rem(lax.div(self.row, 2), 2)
        self.core = lax.rem(self.row, 2)
        self.y = lax.div(self.col, 2)
        self.zl = lax.rem(self.col, 2)


class RowGroup:
    def __init__(self, place):
        self.place = place
        col = place.col
        self.peers = {
            "p": (self.slot(1, 0), col),
            "m": (self.slot(3, 0), col),
            "pair": (self.slot(0, 1), col),
            "sib": (self.slot(0, 0, 1), col),
        }

    def slot(self, ring, pair, sib=0):
        at = self.place
        return (
            lax.rem(at.x + ring, 4) * 4
            + lax.rem(at.zh + pair, 2) * 2
            + lax.rem(at.core + sib, 2)
        )


class ColGroup:
    def __init__(self, place):
        self.place = place
        row = place.row
        self.peers = {
            "p": (row, self.slot(1, 0)),
            "m": (row, self.slot(3, 0)),
            "pair": (row, self.slot(0, 1)),
        }

    def slot(self, ring, pair):
        at = self.place
        return lax.rem(at.y + ring, 4) * 2 + lax.rem(at.zl + pair, 2)


class Wire:
    def __init__(self, send, recv):
        self.send, self.recv = send, recv
        self.names = {}
        self.open = []

    def index(self, name):
        return self.names.setdefault(name, len(self.names))

    def push(self, name, src, dst, to):
        at = self.index(name)
        copy = pltpu.make_async_remote_copy(
            src_ref=src,
            dst_ref=dst,
            send_sem=self.send.at[at],
            recv_sem=self.recv.at[at],
            device_id=to,
            device_id_type=pl.DeviceIdType.MESH,
        )
        copy.start()
        self.open.append(copy)

    def take(self, name, dst, to):
        at = self.index(name)
        pltpu.make_async_remote_copy(
            src_ref=dst,
            dst_ref=dst,
            send_sem=self.send.at[at],
            recv_sem=self.recv.at[at],
            device_id=to,
            device_id_type=pl.DeviceIdType.MESH,
        ).wait_recv()

    def drain(self):
        for copy in self.open:
            copy.wait_send()
        self.open = []


def greet(devices):
    barrier = pltpu.get_barrier_semaphore()
    for device in devices:
        pl.semaphore_signal(barrier, inc=1, device_id=device, device_id_type=pl.DeviceIdType.MESH)
    pl.semaphore_wait(barrier, len(devices))


MOVES = {"p": (3, 0, 0), "m": (1, 0, 0), "pair": (0, 1, 0), "sib": (0, 0, 1)}


def gather(wire, group, buf, tag, src=None):
    rows = buf.shape[1]
    half_rows = rows // 2
    cut = (pl.ds(0, half_rows), pl.ds(half_rows, half_rows))
    has_sib = "sib" in group.peers

    def send(ring, pair, half, way, origin=None):
        ref = buf.at[group.slot(ring, pair), cut[half]]
        dr, dp, dk = MOVES[way]
        name = (tag, (ring + dr) % 4, (pair + dp) % 2, dk, half)
        wire.push(name, ref if origin is None else origin.at[cut[half]], ref, group.peers[way])

    def take(ring, pair, half, sib=0):
        slot = group.slot(ring, pair, 1) if sib else group.slot(ring, pair)
        wire.take((tag, ring, pair, sib, half), buf.at[slot, cut[half]], group.peers["p"])

    def share(ring, pair, half, origin=None):
        if has_sib:
            send(ring, pair, half, "sib", origin)

    send(0, 0, 0, "p", src)
    send(0, 0, 1, "m", src)
    send(0, 0, 0, "pair", src)
    send(0, 0, 1, "p", src)
    send(0, 0, 0, "m", src)
    send(0, 0, 1, "pair", src)
    for half in (0, 1):
        share(0, 0, half, src)
    yield
    take(3, 0, 0)
    send(3, 0, 0, "p")
    take(1, 0, 1)
    send(1, 0, 1, "m")
    share(3, 0, 0)
    share(1, 0, 1)
    yield
    for half in (0, 1):
        take(0, 1, half)
        send(0, 1, half, "p")
        send(0, 1, half, "m")
        share(0, 1, half)
    yield
    take(3, 0, 1)
    take(1, 0, 0)
    share(3, 0, 1)
    share(1, 0, 0)
    yield
    take(3, 1, 0)
    send(3, 1, 0, "p")
    take(1, 1, 1)
    send(1, 1, 1, "m")
    share(3, 1, 0)
    share(1, 1, 1)
    yield
    for half in (0, 1):
        take(2, 0, half)
        share(2, 0, half)
    yield
    take(3, 1, 1)
    take(1, 1, 0)
    share(3, 1, 1)
    share(1, 1, 0)
    for half in (0, 1):
        take(2, 1, half)
        share(2, 1, half)
    yield
    if has_sib:
        for ring in (0, 1, 3, 2):
            for pair in (0, 1):
                for half in (0, 1):
                    take(ring, pair, half, 1)


def add_rows(rows, step, body):
    def one(i, carry):
        body(pl.ds(pl.multiple_of(i * step, step), step))
        return carry

    lax.fori_loop(0, rows // step, one, 0)


def scatter_shapes(rows, width):
    return [
        pltpu.VMEM((2, rows // 2, width), BF16),
        pltpu.VMEM((2, rows // 2, width), BF16),
        pltpu.VMEM((2, rows, width), BF16),
        pltpu.VMEM((2, rows, width), BF16),
        pltpu.VMEM((rows, width), BF16),
    ]


def scatter(wire, group, terms, bufs, tag, prepare):
    relay_m, relay_p, from_m, from_p, from_pair = bufs
    rows = terms.shape[1]
    half_rows = rows // 2
    cut = (pl.ds(0, half_rows), pl.ds(half_rows, half_rows))
    step = 128

    def part(ring, pair, half):
        return terms.at[group.slot(ring, pair), cut[half]]

    def add(target, *others):
        def body(at):
            total = target[at].astype(F32)
            for other in others:
                total = total + other[at].astype(F32)
            target[at] = total.astype(BF16)

        add_rows(half_rows, step, body)

    for q in (1, 0):
        prepare(2, q)
        wire.push((tag, "rm", q), part(2, q, 0), relay_m.at[q], group.peers["p"])
        wire.push((tag, "rp", q), part(2, q, 1), relay_p.at[q], group.peers["m"])
    yield
    for q in (1, 0):
        prepare(1, q)
        prepare(3, q)
        wire.push((tag, "m", q, 1), part(1, q, 1), from_m.at[q, cut[1]], group.peers["p"])
        wire.push((tag, "p", q, 0), part(3, q, 0), from_p.at[q, cut[0]], group.peers["m"])
        yield
        wire.take((tag, "rm", q), relay_m.at[q], group.peers["p"])
        add(part(1, q, 0), relay_m.at[q])
        wire.push((tag, "m", q, 0), part(1, q, 0), from_m.at[q, cut[0]], group.peers["p"])
        wire.take((tag, "rp", q), relay_p.at[q], group.peers["p"])
        add(part(3, q, 1), relay_p.at[q])
        wire.push((tag, "p", q, 1), part(3, q, 1), from_p.at[q, cut[1]], group.peers["m"])
    yield
    prepare(0, 1)
    for half in (0, 1):
        wire.take((tag, "m", 1, half), from_m.at[1, cut[half]], group.peers["p"])
        wire.take((tag, "p", 1, half), from_p.at[1, cut[half]], group.peers["p"])
        add(part(0, 1, half), from_m.at[1, cut[half]], from_p.at[1, cut[half]])
        wire.push((tag, "z", half), part(0, 1, half), from_pair.at[cut[half]], group.peers["pair"])
    yield
    prepare(0, 0)
    for half in (0, 1):
        wire.take((tag, "m", 0, half), from_m.at[0, cut[half]], group.peers["p"])
        wire.take((tag, "p", 0, half), from_p.at[0, cut[half]], group.peers["p"])
    for half in (0, 1):
        wire.take((tag, "z", half), from_pair.at[cut[half]], group.peers["p"])


def run(steps):
    for _ in steps:
        pass


def dot(a, b, dims=((1,), (0,))):
    return lax.dot_general(a, b, (dims, ((), ())), preferred_element_type=F32)


ANY = pl.BlockSpec(memory_space=pl.ANY)
VM = pl.BlockSpec(memory_space=pltpu.VMEM)


def remote_params(collective_id):
    return pltpu.CompilerParams(
        collective_id=collective_id, has_side_effects=True, vmem_limit_bytes=VMEM_LIMIT
    )


def node_gather_kernel(nodes, out, send, recv, own_sem):
    group = RowGroup(Place())
    greet(list(group.peers.values()))
    own = pltpu.make_async_copy(nodes, out.at[group.slot(0, 0)], own_sem)
    own.start()
    wire = Wire(send, recv)
    run(gather(wire, group, out, "n", nodes))
    wire.drain()
    own.wait()


def node_gather(nodes):
    rows, width = nodes.shape
    return pl.pallas_call(
        node_gather_kernel,
        out_shape=jax.ShapeDtypeStruct((16, rows, width), BF16),
        in_specs=[ANY],
        out_specs=ANY,
        scratch_shapes=[
            pltpu.SemaphoreType.DMA((30,)),
            pltpu.SemaphoreType.DMA((30,)),
            pltpu.SemaphoreType.DMA,
        ],
        compiler_params=remote_params(1),
        name="node_gather",
    )(nodes)


def forward_kernel(cols, count, tiles, nodes, out):
    step = pl.program_id(0)
    per = tiles.shape[0]
    for i in range(per):
        at = step * per + i
        live = count[at]
        base = pl.ds(i * 128, 128)

        @pl.when(live <= 2)
        def _():
            pair = jnp.concatenate(
                [jnp.where(k < live, tiles[i, k], jnp.zeros((), BF16)) for k in (0, 1)], axis=1
            )
            picked = jnp.concatenate([nodes[cols[at, k]] for k in (0, 1)], axis=0)
            out[base] = dot(pair, picked).astype(BF16)

        @pl.when(live > 2)
        def _():
            four = jnp.concatenate(
                [jnp.where(k < live, tiles[i, k], jnp.zeros((), BF16)) for k in range(4)], axis=1
            )
            picked = jnp.concatenate([nodes[cols[at, k]] for k in range(4)], axis=0)
            out[base] = dot(four, picked).astype(BF16)


def forward(cols, count, tiles, nodes):
    row_blocks = tiles.shape[0]
    width = nodes.shape[-1]
    per = 8
    return pl.pallas_call(
        forward_kernel,
        out_shape=jax.ShapeDtypeStruct((row_blocks * 128, width), BF16),
        grid_spec=pltpu.PrefetchScalarGridSpec(
            num_scalar_prefetch=2,
            grid=(row_blocks // per,),
            in_specs=[
                pl.BlockSpec((per, 4, 128, 128), lambda s, *_: (s, 0, 0, 0)),
                pl.BlockSpec(nodes.shape, lambda s, *_: (0, 0, 0)),
            ],
            out_specs=pl.BlockSpec((per * 128, width), lambda s, *_: (s, 0)),
        ),
        compiler_params=pltpu.CompilerParams(vmem_limit_bytes=VMEM_LIMIT),
        name="forward",
    )(cols, count, tiles, nodes)


def middle_kernel(
    partial, nodes, cot, w_in, bias, w_out, gain, shift,
    grads, updated, direct, gw_in, gw_out, gvec,
    terms, relay_m, relay_p, from_m, from_p, from_pair,
    msg_s, act_s, gproj_s, gpre_s, send, recv, load,
):
    group = ColGroup(Place())
    width = nodes.shape[1]
    rows = nodes.shape[0]

    def loader(ring, pair):
        slot = group.slot(ring, pair)
        return pltpu.make_async_copy(partial.at[slot], terms.at[slot], load.at[ring * 2 + pair])

    for ring in (2, 1, 3, 0):
        for pair in (1, 0):
            loader(ring, pair).start()
    greet(list(group.peers.values()))
    wire = Wire(send, recv)
    bufs = (relay_m, relay_p, from_m, from_p, from_pair)
    run(scatter(wire, group, terms, bufs, "s", lambda ring, pair: loader(ring, pair).wait()))
    own = group.slot(0, 0)
    gvec[...] = jnp.zeros_like(gvec)

    def chunk(i, carry):
        at = pl.ds(pl.multiple_of(i * 256, 256), 256)
        msg = (
            terms[own, at].astype(F32)
            + from_m[0, at].astype(F32)
            + from_p[0, at].astype(F32)
            + from_pair[at].astype(F32)
        ).astype(BF16)
        msg_s[at] = msg
        mine = nodes[at]
        pre = dot(mine, w_in[:width]) + dot(msg, w_in[width:]) + bias[...]
        sig = jax.nn.sigmoid(pre)
        act = (pre * sig).astype(BF16)
        act_s[at] = act
        proj = dot(act, w_out[...])
        mean = jnp.mean(proj, axis=-1, keepdims=True)
        off = proj - mean
        var = jnp.mean(off * off, axis=-1, keepdims=True)
        rstd = 1.0 / jnp.sqrt(var + EPS)
        normed = off * rstd
        updated[at] = (mine.astype(F32) + normed * gain[...] + shift[...]).astype(BF16)
        grad_out = cot[at].astype(F32)
        gscaled = grad_out * gain[...]
        gproj = (
            (
                gscaled
                - jnp.mean(gscaled, axis=-1, keepdims=True)
                - normed * jnp.mean(gscaled * normed, axis=-1, keepdims=True)
            )
            * rstd
        ).astype(BF16)
        gproj_s[at] = gproj
        gact = dot(gproj, w_out[...], ((1,), (1,)))
        gpre = gact * sig * (1.0 + pre * (1.0 - sig))
        gpre_b = gpre.astype(BF16)
        gpre_s[at] = gpre_b
        grads[own, at] = dot(gpre_b, w_in[width:], ((1,), (1,))).astype(BF16)
        direct[at] = grad_out + dot(gpre_b, w_in[:width], ((1,), (1,)))
        gvec[0:1] += jnp.sum(gpre, axis=0, keepdims=True)
        gvec[1:2] += jnp.sum(grad_out * normed, axis=0, keepdims=True)
        gvec[2:3] += jnp.sum(grad_out, axis=0, keepdims=True)
        return carry

    lax.fori_loop(0, rows // 256, chunk, 0)
    steps = gather(wire, group, grads, "g")
    next(steps)
    gw_in[:width] = dot(nodes[...], gpre_s[...], ((0,), (0,)))
    gw_in[width:] = dot(msg_s[...], gpre_s[...], ((0,), (0,)))
    gw_out[...] = dot(act_s[...], gproj_s[...], ((0,), (0,)))
    run(steps)
    wire.drain()


def middle(partial, nodes, cot, w_in, bias, w_out, gain, shift):
    rows, width = nodes.shape
    one = functools.partial(pltpu.VMEM, (rows, width))
    return pl.pallas_call(
        middle_kernel,
        out_shape=[
            jax.ShapeDtypeStruct((8, rows, width), BF16),
            jax.ShapeDtypeStruct((rows, width), BF16),
            jax.ShapeDtypeStruct((rows, width), F32),
            jax.ShapeDtypeStruct((2 * width, width), F32),
            jax.ShapeDtypeStruct((width, width), F32),
            jax.ShapeDtypeStruct((3, width), F32),
        ],
        in_specs=[ANY] + [VM] * 7,
        out_specs=[VM] * 6,
        scratch_shapes=[pltpu.VMEM((8, rows, width), BF16)]
        + scatter_shapes(rows, width)
        + [one(BF16)] * 4
        + [
            pltpu.SemaphoreType.DMA((40,)),
            pltpu.SemaphoreType.DMA((40,)),
            pltpu.SemaphoreType.DMA((8,)),
        ],
        compiler_params=remote_params(2),
        name="middle",
    )(partial.reshape(8, rows, width), nodes, cot, w_in, bias, w_out, gain, shift)


def backward_kernel(cols, count, tiles, nodes, grads, tile_grads, back, acc):
    step = pl.program_id(0)
    per = tiles.shape[0]

    @pl.when(step == 0)
    def _():
        def clear(i, carry):
            acc[i] = jnp.zeros(acc.shape[1:], F32)
            return carry

        lax.fori_loop(0, acc.shape[0], clear, 0)

    scale = F32(256.0) ** F32(-0.5)
    for i in range(per):
        at = step * per + i
        live = count[at]
        base = pl.ds(i * 128, 128)
        for k in range(4):
            @pl.when(k < live)
            def _():
                col = cols[at, k]
                grad = grads[base]
                tile_grads[i, k] = (dot(grad, nodes[col], ((1,), (1,))) * scale).astype(BF16)
                acc[col] += dot(tiles[i, k], grad, ((0,), (0,)))

            @pl.when(k >= live)
            def _():
                tile_grads[i, k] = jnp.zeros((128, 128), BF16)

    @pl.when(step == pl.num_programs(0) - 1)
    def _():
        def put(i, carry):
            back[i] = acc[i].astype(BF16)
            return carry

        lax.fori_loop(0, acc.shape[0], put, 0)


def backward(cols, count, tiles, nodes, grads):
    row_blocks = tiles.shape[0]
    blocks, _, width = nodes.shape
    per = 8
    return pl.pallas_call(
        backward_kernel,
        out_shape=[
            jax.ShapeDtypeStruct(tiles.shape, BF16),
            jax.ShapeDtypeStruct(nodes.shape, BF16),
        ],
        grid_spec=pltpu.PrefetchScalarGridSpec(
            num_scalar_prefetch=2,
            grid=(row_blocks // per,),
            in_specs=[
                pl.BlockSpec((per, 4, 128, 128), lambda s, *_: (s, 0, 0, 0)),
                pl.BlockSpec(nodes.shape, lambda s, *_: (0, 0, 0), pipeline_mode=pl.Buffered(1)),
                pl.BlockSpec((per * 128, width), lambda s, *_: (s, 0)),
            ],
            out_specs=[
                pl.BlockSpec((per, 4, 128, 128), lambda s, *_: (s, 0, 0, 0)),
                pl.BlockSpec(nodes.shape, lambda s, *_: (0, 0, 0), pipeline_mode=pl.Buffered(1)),
            ],
            scratch_shapes=[pltpu.VMEM(nodes.shape, F32)],
        ),
        compiler_params=pltpu.CompilerParams(vmem_limit_bytes=VMEM_LIMIT),
        name="backward",
    )(cols, count, tiles, nodes, grads)


def finish_kernel(
    back, direct, out,
    terms, others, relay_m, relay_p, from_m, from_p, from_pair, send, recv, load,
):
    group = RowGroup(Place())
    rows = terms.shape[1]
    order = [(2, 1), (2, 0), (1, 1), (3, 1), (1, 0), (3, 0), (0, 1), (0, 0)]

    def loader(ring, pair):
        slot = group.slot(ring, pair)
        return pltpu.make_async_copy(back.at[slot], terms.at[slot], load.at[ring * 2 + pair])

    for at in order:
        loader(*at).start()
    greet(list(group.peers.values()))
    wire = Wire(send, recv)
    for ring, pair in order:
        wire.push(
            ("f", ring, pair),
            back.at[group.slot(ring, pair, 1)],
            others.at[ring * 2 + pair],
            group.peers["sib"],
        )

    def prepare(ring, pair):
        loader(ring, pair).wait()
        other = others.at[ring * 2 + pair]
        wire.take(("f", ring, pair), other, group.peers["sib"])
        slot = group.slot(ring, pair)

        def body(at):
            terms[slot, at] = (terms[slot, at].astype(F32) + other[at].astype(F32)).astype(BF16)

        add_rows(rows, 128, body)

    bufs = (relay_m, relay_p, from_m, from_p, from_pair)
    run(scatter(wire, group, terms, bufs, "b", prepare))
    own = group.slot(0, 0)

    def last(at):
        out[at] = (
            direct[at]
            + terms[own, at].astype(F32)
            + from_m[0, at].astype(F32)
            + from_p[0, at].astype(F32)
            + from_pair[at].astype(F32)
        ).astype(BF16)

    add_rows(rows, 128, last)
    wire.drain()


def finish(back, direct):
    rows, width = direct.shape
    return pl.pallas_call(
        finish_kernel,
        out_shape=jax.ShapeDtypeStruct((rows, width), BF16),
        in_specs=[ANY, VM],
        out_specs=VM,
        scratch_shapes=[
            pltpu.VMEM((16, rows, width), BF16),
            pltpu.VMEM((8, rows, width), BF16),
        ]
        + scatter_shapes(rows, width)
        + [
            pltpu.SemaphoreType.DMA((40,)),
            pltpu.SemaphoreType.DMA((40,)),
            pltpu.SemaphoreType.DMA((8,)),
        ],
        compiler_params=remote_params(3),
        name="finish",
    )(back.reshape(16, rows, width), direct)


def body(nodes, tiles, tile_col, tile_count, w_in, bias_in, w_out, ln_gain, ln_shift, cotangent):
    rows, width = nodes.shape
    cols, count = tile_col[:, 0], tile_count[:, 0]
    slots = tiles[:, 0]
    cols = jnp.clip(cols, 0, 127)
    gathered = node_gather(nodes).reshape(128, 128, width)
    partial = forward(cols, count, slots, gathered)
    grads, updated, direct, gw_in, gw_out, gvec = middle(
        partial, nodes, cotangent, w_in, bias_in[None], w_out, ln_gain[None], ln_shift[None]
    )
    gw_in, gw_out, gvec = lax.psum((gw_in, gw_out, gvec), ("row", "col"))
    grad_tiles, back = backward(cols, count, slots, gathered, grads.reshape(8 * rows, width))
    grad_nodes = finish(back, direct)
    total_nodes = rows * lax.axis_size("row") * lax.axis_size("col")
    factor = jnp.float32(total_nodes) ** (-0.5)
    return (
        updated,
        grad_nodes,
        grad_tiles[:, None],
        gw_in * factor,
        gw_out * factor,
        gvec * factor,
    )


def solution(mesh):
    placed = (
        P(("row", "col"), None),
        P("row", "col", None, None, None),
        P("row", "col", None),
        P("row", "col"),
        P(),
        P(),
        P(),
        P(),
        P(),
        P(("row", "col"), None),
    )
    return jax.shard_map(
        body,
        mesh=mesh,
        in_specs=placed,
        out_specs=(
            P(("row", "col"), None),
            P(("row", "col"), None),
            P("row", "col", None, None, None),
            P(),
            P(),
            P(),
        ),
        check_vma=False,
    )
```

time: 577 us -> 320 us (0.55); the launches traced: 569 us -> 319 us
  waiting for transfers between devices: 259 us -> 0.02 us
  Pallas kernels: 0 us -> 229 us
  other arithmetic: 91 us -> 4.77 us
  local copies, waits for them, and re-layouts: 85.2 us -> 3.44 us
  matrix products: 49.8 us -> 0 us
    pallas_call x0 -> x5, Pallas kernels: none -> 229 us  [the longest x1 84 us: middle(): pl.pallas_call(middle_kernel, out_shape=[jax.ShapeDtypeStruct((8, rows, w...]
    all_gather x2 -> x0, waiting for transfers between devices: 164 us -> none  [the longest x1 86.6 us: body(): lax.all_gather(gmsg, 'col', axis=0, tiled=True)]
    reduce_scatter x2 -> x0, waiting for transfers between devices: 94.4 us -> none  [the longest x1 86.9 us: body(): lax.psum_scatter(partial_value.reshape(row_blocks * block, width).astype(...]
    scatter-add x1 -> x0, other arithmetic: 73.3 us -> none  [body(): jax.ops.segment_sum(flat_back, flat_cols, num_segments=col_blocks)]
    dot_general x12 -> x0, matrix products: 49.8 us -> none  [the longest x1 17.7 us: body(): jnp.einsum('rkij,rid->rkjd', live_tiles, grad_rows, preferred_element_typ...]
    unnamed x27 -> x7, local copies, waits for them, and re-layouts: 46.3 us -> 3.44 us
    reshape x2 -> x0, local copies, waits for them, and re-layouts: 25.4 us -> none  [body(): column_terms.reshape(col_blocks * block, width)]
    gather x1 -> x0, local copies, waits for them, and re-layouts: 13.2 us -> none  [pick_blocks(): return blocks[cols]]
  transfers between devices with their start and end apart: 5 -> 1, of which waited for: 4 -> 0; matrix products, arithmetic and copies ran while one was open for 34% -> 0% of each run, Pallas kernels for 0% -> 26%
where the time goes in v1:
time: 320 us; the launch traced here: 319 us
  Pallas kernels  229 us (72%)
  blocking collectives  67.9 us (21%)
  between operations  14.1 us (4%)
  other arithmetic  4.77 us (1%)
  local copies, waits for them, and re-layouts  3.44 us (1%)
    pallas_call x1, Pallas kernels, middle(): pl.pallas_call(middle_kernel, out_shape=[jax.ShapeDtypeStruct((8, rows, w...  84 us
    psum x1, blocking collectives, body(): gw_in, gw_out, gvec = lax.psum((gw_in, gw_out, gvec), ('row', 'col'))  67.9 us
    pallas_call x1, Pallas kernels, node_gather(): pl.pallas_call(node_gather_kernel, out_shape=jax.ShapeDtypeStruct((16, ro...  44.9 us
    pallas_call x1, Pallas kernels, finish(): pl.pallas_call(finish_kernel, out_shape=jax.ShapeDtypeStruct((rows, width...  42.5 us
    pallas_call x1, Pallas kernels, backward(): pl.pallas_call(backward_kernel, out_shape=[jax.ShapeDtypeStruct(tiles.sha...  39.5 us
    pallas_call x1, Pallas kernels, forward(): pl.pallas_call(forward_kernel, out_shape=jax.ShapeDtypeStruct((row_blocks...  17.7 us
  transfers between devices with their start and end apart: 1, of which 0 were waited for; matrix products, arithmetic and copies ran while one was open for 0% of the time, Pallas kernels for 26%

profile of v1, /device:TPU:1, one launch (start us, length us, event | category | flops | bytes accessed | tf_op | source)
XLA Modules:
  0.0 318.8 jit_solution(5358675441260234138)
XLA Ops:
  7.2 0.0 all-reduce.3.cloned.1.call-start
  7.2 0.8 copy.16
  8.0 0.6 clamp_bitcast_fusion.cols
  8.6 44.9 %node_gather.1 = bf16[16,1024,256]{2,1,0:T(8,128)(2,1)} custom-call(bf16[1024,256]{1,0:T(8,128)(2,1)} %nodes.3), custom_call_target="tpu_custom_call" | custom-call | tf_op jit(solution)/shard_map/node_gather/pallas_call | solution.py:286
  53.5 17.7 %forward.1 = bf16[8192,256]{1,0:T(8,128)(2,1)} custom-call(s32[64,4]{1,0:T(8,128)} %clamp_bitcast_fusion.cols, s32[64]{0:T(128)} %bitcast.21, bf16[64,4,128,128]{3,2,1,0:T(8,128)(2,1)} %bitcast.16, bf16[128,128,256]{2,1,0:T(8,128)(2,1)} %bitcast.14), custom_call_target="tpu_custom_call" | custom-call | tf_op jit(solution)/shard_map/forward/pallas_call | solution.py:330
  71.2 84.0 %middle.1 = (bf16[8,1024,256]{2,1,0:T(8,128)(2,1)}, bf16[1024,256]{1,0:T(8,128)(2,1)}, f32[1024,256]{1,0:T(8,128)}, f32[512,256]{1,0:T(8,128)}, f32[256,256]{1,0:T(8,128)}, /*index=5*/f32[3,256]{1,0:T(4,128)}) custom-call(bf16[8,1024,256]{2,1,0:T(8,128)(2,1)} %bitcast.18, bf16[1024,256]{1,0:T(8,128)(2,1)} %nodes.3, bf16[1024,256]{1,0:T(8,128)(2,1)} %cot.1, ...), custom_call_target="tpu_custom_call" | custom-call | tf_op jit(solution)/shard_map/middle/pallas_call | solution.py:427
  155.2 0.0 all-reduce.3.cloned.1.call-update
  155.3 39.5 %backward.1 = (bf16[64,4,128,128]{3,2,1,0:T(8,128)(2,1)}, bf16[128,128,256]{2,1,0:T(8,128)(2,1)}) custom-call(s32[64,4]{1,0:T(8,128)} %clamp_bitcast_fusion.cols, s32[64]{0:T(128)} %bitcast.22, bf16[64,4,128,128]{3,2,1,0:T(8,128)(2,1)} %bitcast.17, bf16[128,128,256]{2,1,0:T(8,128)(2,1)} %bitcast.15, bf16[8192,256]{1,0:T(8,128)(2,1)} %bitcast.20), custom_call_target="tpu_custom_call" | custom-call | tf_op jit(solution)/shard_map/backward/pallas_call | solution.py:494
  194.8 0.0 copy-start.1
  194.8 0.0 copy-start
  194.8 42.5 %finish.1 = bf16[1024,256]{1,0:T(8,128)(2,1)} custom-call(bf16[16,1024,256]{2,1,0:T(8,128)(2,1)} %bitcast.19, f32[1024,256]{1,0:T(8,128)} %get-tuple-element.17.direct), custom_call_target="tpu_custom_call" | custom-call | tf_op jit(solution)/shard_map/finish/pallas_call | solution.py:573
  237.3 0.0 copy-done.1
  237.3 67.9 %psum.23 = f32[3,256]{1,0:T(4,128)S(1)} all-reduce(f32[3,256]{1,0:T(4,128)S(1)} %copy-done.1), channel_id=1, replica_groups=mesh['row'=16,'col'=8] {'row','col'}, use_global_device_ids=true, to_apply=%region_2.3 | all-reduce | flops 768 | bytes 6144 | tf_op jit(solution)/shard_map/psum | solution.py:603
  305.2 0.6 broadcast_multiply_fusion.2
  305.8 0.0 all-reduce.3.cloned.1.call-done
  305.8 1.9 broadcast_multiply_fusion
  307.7 1.7 broadcast_multiply_fusion.1
  309.3 0.0 copy-done
  309.3 0.8 copy.22
  310.1 1.9 copy.23
Async XLA Ops:
  7.2 298.6 %all-reduce.3.cloned.1.call-start = ((), (), s32[]{:S(2)}) async-start(), calls=%async_computation | async-start | bytes 1572864 | tf_op jit(solution)/shard_map/psum | solution.py:603
  194.8 42.5 %copy-start.1 = (f32[3,256]{1,0:T(4,128)S(1)}, f32[3,256]{1,0:T(4,128)}, u32[]{:S(2)}) copy-start(f32[3,256]{1,0:T(4,128)} %get-tuple-element.21) | copy-start | bytes 9220
  194.8 114.5 %copy-start = (bf16[1024,256]{1,0:T(8,128)(2,1)S(1)}, bf16[1024,256]{1,0:T(8,128)(2,1)}, u32[]{:S(2)}) copy-start(bf16[1024,256]{1,0:T(8,128)(2,1)} %get-tuple-element.36) | copy-start | bytes 1572868
Sparse Core Ops, SparseCore 0:
  155.4 146.6 all-reduce.2

commit v2 on v1

--- a/solution.py
+++ b/solution.py
@@ -11,6 +11,7 @@
 MIB = 1024 * 1024
 VMEM_LIMIT = 56 * MIB
 EPS = 1e-05
+TOTAL_ROWS = 1024
 
 
 class Place:
@@ -22,6 +23,16 @@
         self.core = lax.rem(self.row, 2)
         self.y = lax.div(self.col, 2)
         self.zl = lax.rem(self.col, 2)
+
+
+    def peer(self, x=0, y=0, z=0, core=0):
+        z_at = lax.rem(self.zh * 2 + self.zl + z, 4)
+        row = lax.rem(self.x + x, 4) * 4 + lax.div(z_at, 2) * 2 + lax.rem(self.core + core, 2)
+        return (row, lax.rem(self.y + y, 4) * 2 + lax.rem(z_at, 2))
+
+    def all_peers(self):
+        steps = [dict(core=1)] + [{axis: d} for axis in "xyz" for d in (1, 2, 3)]
+        return [self.peer(**step) for step in steps]
 
 
 class RowGroup:
@@ -249,6 +260,79 @@
         wire.take((tag, "p", 0, half), from_p.at[0, cut[half]], group.peers["p"])
     for half in (0, 1):
         wire.take((tag, "z", half), from_pair.at[cut[half]], group.peers["p"])
+
+
+def total_shapes(width):
+    return [
+        pltpu.VMEM((TOTAL_ROWS, width), F32),
+        pltpu.VMEM((TOTAL_ROWS // 2, width), F32),
+        pltpu.VMEM((3, TOTAL_ROWS // 8, width), F32),
+        pltpu.VMEM((3, TOTAL_ROWS // 32, width), F32),
+        pltpu.VMEM((4, TOTAL_ROWS // 32, width), F32),
+    ]
+
+
+def total(wire, place, mine, bufs, tag):
+    result, in_core, in_x, in_y, in_z = bufs
+    half, quarter, piece = TOTAL_ROWS // 2, TOTAL_ROWS // 8, TOTAL_ROWS // 32
+
+    def span(core, x=None, y=None):
+        start, size = core * half, half
+        if x is not None:
+            start, size = start + x * quarter, quarter
+        if y is not None:
+            start, size = start + y * piece, piece
+        return pl.ds(pl.multiple_of(start, piece), size)
+
+    core, x, y = place.core, place.x, place.y
+    z = place.zh * 2 + place.zl
+    other = 1 - core
+    sib = place.peer(core=1)
+    wire.push((tag, "core"), mine.at[span(other)], in_core, sib)
+    yield
+    wire.take((tag, "core"), in_core, sib)
+
+    def fold(i, carry):
+        at = pl.ds(pl.multiple_of(core * half + i * 64, 64), 64)
+        mine[at] += in_core[pl.ds(pl.multiple_of(i * 64, 64), 64)]
+        return carry
+
+    lax.fori_loop(0, half // 64, fold, 0)
+    for d in (1, 2, 3):
+        to = place.peer(x=d)
+        wire.push((tag, "x", d), mine.at[span(core, lax.rem(x + d, 4))], in_x.at[d - 1], to)
+    yield
+    for d in (1, 2, 3):
+        wire.take((tag, "x", d), in_x.at[d - 1], sib)
+    mine[span(core, x)] += in_x[0] + in_x[1] + in_x[2]
+    for d in (1, 2, 3):
+        to = place.peer(y=d)
+        wire.push((tag, "y", d), mine.at[span(core, x, lax.rem(y + d, 4))], in_y.at[d - 1], to)
+    yield
+    for d in (1, 2, 3):
+        wire.take((tag, "y", d), in_y.at[d - 1], sib)
+    in_z[z] = mine[span(core, x, y)] + in_y[0] + in_y[1] + in_y[2]
+    for d in (1, 2, 3):
+        wire.push((tag, "z", d), in_z.at[z], in_z.at[z], place.peer(z=d))
+    yield
+    for d in (1, 2, 3):
+        wire.take((tag, "z", d), in_z.at[lax.rem(z + 4 - d, 4)], sib)
+    at = span(core, x, y)
+    result[at] = in_z[0] + in_z[1] + in_z[2] + in_z[3]
+    for d in (1, 2, 3):
+        wire.push((tag, "back y", d), result.at[at], result.at[at], place.peer(y=d))
+    yield
+    for d in (1, 2, 3):
+        wire.take((tag, "back y", d), result.at[span(core, x, lax.rem(y + 4 - d, 4))], sib)
+    at = span(core, x)
+    for d in (1, 2, 3):
+        wire.push((tag, "back x", d), result.at[at], result.at[at], place.peer(x=d))
+    yield
+    for d in (1, 2, 3):
+        wire.take((tag, "back x", d), result.at[span(core, lax.rem(x + 4 - d, 4))], sib)
+    wire.push((tag, "back core"), result.at[span(core)], result.at[span(core)], sib)
+    yield
+    wire.take((tag, "back core"), result.at[span(other)], sib)
 
 
 def run(steps):
@@ -346,7 +430,7 @@
 
 def middle_kernel(
     partial, nodes, cot, w_in, bias, w_out, gain, shift,
-    grads, updated, direct, gw_in, gw_out, gvec,
+    grads, updated, direct, weights,
     terms, relay_m, relay_p, from_m, from_p, from_pair,
     msg_s, act_s, gproj_s, gpre_s, send, recv, load,
 ):
@@ -366,7 +450,8 @@
     bufs = (relay_m, relay_p, from_m, from_p, from_pair)
     run(scatter(wire, group, terms, bufs, "s", lambda ring, pair: loader(ring, pair).wait()))
     own = group.slot(0, 0)
-    gvec[...] = jnp.zeros_like(gvec)
+    gvec = weights.at[pl.ds(3 * width, 8)]
+    weights[3 * width :] = jnp.zeros((weights.shape[0] - 3 * width, width), F32)
 
     def chunk(i, carry):
         at = pl.ds(pl.multiple_of(i * 256, 256), 256)
@@ -414,9 +499,9 @@
     lax.fori_loop(0, rows // 256, chunk, 0)
     steps = gather(wire, group, grads, "g")
     next(steps)
-    gw_in[:width] = dot(nodes[...], gpre_s[...], ((0,), (0,)))
-    gw_in[width:] = dot(msg_s[...], gpre_s[...], ((0,), (0,)))
-    gw_out[...] = dot(act_s[...], gproj_s[...], ((0,), (0,)))
+    weights[:width] = dot(nodes[...], gpre_s[...], ((0,), (0,)))
+    weights[width : 2 * width] = dot(msg_s[...], gpre_s[...], ((0,), (0,)))
+    weights[2 * width : 3 * width] = dot(act_s[...], gproj_s[...], ((0,), (0,)))
     run(steps)
     wire.drain()
 
@@ -430,12 +515,10 @@
             jax.ShapeDtypeStruct((8, rows, width), BF16),
             jax.ShapeDtypeStruct((rows, width), BF16),
             jax.ShapeDtypeStruct((rows, width), F32),
-            jax.ShapeDtypeStruct((2 * width, width), F32),
-            jax.ShapeDtypeStruct((width, width), F32),
-            jax.ShapeDtypeStruct((3, width), F32),
+            jax.ShapeDtypeStruct((TOTAL_ROWS, width), F32),
         ],
         in_specs=[ANY] + [VM] * 7,
-        out_specs=[VM] * 6,
+        out_specs=[VM] * 4,
         scratch_shapes=[pltpu.VMEM((8, rows, width), BF16)]
         + scatter_shapes(rows, width)
         + [one(BF16)] * 4
@@ -517,10 +600,12 @@
 
 
 def finish_kernel(
-    back, direct, out,
-    terms, others, relay_m, relay_p, from_m, from_p, from_pair, send, recv, load,
+    back, direct, weights, out, gw_in, gw_out, gvec,
+    terms, others, relay_m, relay_p, from_m, from_p, from_pair,
+    mine, result, in_core, in_x, in_y, in_z, send, recv, load,
 ):
-    group = RowGroup(Place())
+    place = Place()
+    group = RowGroup(place)
     rows = terms.shape[1]
     order = [(2, 1), (2, 0), (1, 1), (3, 1), (1, 0), (3, 0), (0, 1), (0, 0)]
 
@@ -528,10 +613,15 @@
         slot = group.slot(ring, pair)
         return pltpu.make_async_copy(back.at[slot], terms.at[slot], load.at[ring * 2 + pair])
 
+    whole = pltpu.make_async_copy(weights, mine, load.at[8])
+    whole.start()
     for at in order:
         loader(*at).start()
-    greet(list(group.peers.values()))
+    greet(place.all_peers())
     wire = Wire(send, recv)
+    whole.wait()
+    sums = total(wire, place, mine, (result, in_core, in_x, in_y, in_z), "w")
+    next(sums)
     for ring, pair in order:
         wire.push(
             ("f", ring, pair),
@@ -552,7 +642,8 @@
         add_rows(rows, 128, body)
 
     bufs = (relay_m, relay_p, from_m, from_p, from_pair)
-    run(scatter(wire, group, terms, bufs, "b", prepare))
+    for _ in scatter(wire, group, terms, bufs, "b", prepare):
+        next(sums, None)
     own = group.slot(0, 0)
 
     def last(at):
@@ -565,29 +656,42 @@
         ).astype(BF16)
 
     add_rows(rows, 128, last)
+    run(sums)
+    width = out.shape[1]
+    factor = F32(131072.0) ** F32(-0.5)
+    gw_in[...] = result[: 2 * width] * factor
+    gw_out[...] = result[2 * width : 3 * width] * factor
+    gvec[...] = result[3 * width : 3 * width + 3] * factor
     wire.drain()
 
 
-def finish(back, direct):
+def finish(back, direct, weights):
     rows, width = direct.shape
     return pl.pallas_call(
         finish_kernel,
-        out_shape=jax.ShapeDtypeStruct((rows, width), BF16),
-        in_specs=[ANY, VM],
-        out_specs=VM,
+        out_shape=[
+            jax.ShapeDtypeStruct((rows, width), BF16),
+            jax.ShapeDtypeStruct((2 * width, width), F32),
+            jax.ShapeDtypeStruct((width, width), F32),
+            jax.ShapeDtypeStruct((3, width), F32),
+        ],
+        in_specs=[ANY, VM, ANY],
+        out_specs=[VM] * 4,
         scratch_shapes=[
             pltpu.VMEM((16, rows, width), BF16),
             pltpu.VMEM((8, rows, width), BF16),
         ]
         + scatter_shapes(rows, width)
+        + [pltpu.VMEM((TOTAL_ROWS, width), F32)]
+        + total_shapes(width)
         + [
-            pltpu.SemaphoreType.DMA((40,)),
-            pltpu.SemaphoreType.DMA((40,)),
-            pltpu.SemaphoreType.DMA((8,)),
+            pltpu.SemaphoreType.DMA((60,)),
+            pltpu.SemaphoreType.DMA((60,)),
+            pltpu.SemaphoreType.DMA((9,)),
         ],
         compiler_params=remote_params(3),
         name="finish",
-    )(back.reshape(16, rows, width), direct)
+    )(back.reshape(16, rows, width), direct, weights)
 
 
 def body(nodes, tiles, tile_col, tile_count, w_in, bias_in, w_out, ln_gain, ln_shift, cotangent):
@@ -597,22 +701,12 @@
     cols = jnp.clip(cols, 0, 127)
     gathered = node_gather(nodes).reshape(128, 128, width)
     partial = forward(cols, count, slots, gathered)
-    grads, updated, direct, gw_in, gw_out, gvec = middle(
+    grads, updated, direct, weights = middle(
         partial, nodes, cotangent, w_in, bias_in[None], w_out, ln_gain[None], ln_shift[None]
     )
-    gw_in, gw_out, gvec = lax.psum((gw_in, gw_out, gvec), ("row", "col"))
     grad_tiles, back = backward(cols, count, slots, gathered, grads.reshape(8 * rows, width))
-    grad_nodes = finish(back, direct)
-    total_nodes = rows * lax.axis_size("row") * lax.axis_size("col")
-    factor = jnp.float32(total_nodes) ** (-0.5)
-    return (
-        updated,
-        grad_nodes,
-        grad_tiles[:, None],
-        gw_in * factor,
-        gw_out * factor,
-        gvec * factor,
-    )
+    grad_nodes, gw_in, gw_out, gvec = finish(back, direct, weights)
+    return updated, grad_nodes, grad_tiles[:, None], gw_in, gw_out, gvec
 
 
 def solution(mesh):

time: 320 us -> 257 us (0.80)
  blocking collectives: 67.9 us -> 0 us
  Pallas kernels: 229 us -> 245 us
  between operations: 14.1 us -> 0.67 us
  local copies, waits for them, and re-layouts: 3.44 us -> 8.25 us
  other arithmetic: 4.77 us -> 0.62 us
    psum x1 -> x0, blocking collectives: 67.9 us -> none  [body(): gw_in, gw_out, gvec = lax.psum((gw_in, gw_out, gvec), ('row', 'col'))]
    pallas_call x1, Pallas kernels: 42.5 us -> 59.7 us  [finish(): pl.pallas_call(finish_kernel, out_shape=[jax.ShapeDtypeStruct((rows, widt...]
    unnamed x7 -> x8, local copies, waits for them, and re-layouts: 3.44 us -> 8.25 us
    mul x3 -> x0, other arithmetic: 4.15 us -> none  [the longest x1 1.88 us: body(): gw_in * factor]
  transfers between devices with their start and end apart: 1 -> 0, of which waited for: 0 -> 0; matrix products, arithmetic and copies ran while one was open for 0% -> 0% of each run, Pallas kernels for 26% -> 0%
where the time goes in v2:
time: 257 us; the launch traced here: 254 us
  Pallas kernels  245 us (95%)
  local copies, waits for them, and re-layouts  8.25 us (3%)
    pallas_call x1, Pallas kernels, middle(): pl.pallas_call(middle_kernel, out_shape=[jax.ShapeDtypeStruct((8, rows, w...  82.5 us
    pallas_call x1, Pallas kernels, finish(): pl.pallas_call(finish_kernel, out_shape=[jax.ShapeDtypeStruct((rows, widt...  59.7 us
    pallas_call x1, Pallas kernels, node_gather(): pl.pallas_call(node_gather_kernel, out_shape=jax.ShapeDtypeStruct((16, ro...  44.9 us
    pallas_call x1, Pallas kernels, backward(): pl.pallas_call(backward_kernel, out_shape=[jax.ShapeDtypeStruct(tiles.sha...  39.7 us
    pallas_call x1, Pallas kernels, forward(): pl.pallas_call(forward_kernel, out_shape=jax.ShapeDtypeStruct((row_blocks...  17.7 us
    unnamed x8, local copies, waits for them, and re-layouts  8.25 us

profile of v2, /device:TPU:1, one launch (start us, length us, event | category | flops | bytes accessed | tf_op | source)
XLA Modules:
  0.0 254.0 jit_solution(952463821924126094)
XLA Ops:
  0.6 0.8 copy.16
  1.4 0.6 clamp_bitcast_fusion.cols
  2.0 44.9 %node_gather.1 = bf16[16,1024,256]{2,1,0:T(8,128)(2,1)} custom-call(bf16[1024,256]{1,0:T(8,128)(2,1)} %nodes.3), custom_call_target="tpu_custom_call" | custom-call | tf_op jit(solution)/shard_map/node_gather/pallas_call | solution.py:370
  46.9 17.7 %forward.1 = bf16[8192,256]{1,0:T(8,128)(2,1)} custom-call(s32[64,4]{1,0:T(8,128)} %clamp_bitcast_fusion.cols, s32[64]{0:T(128)} %bitcast.21, bf16[64,4,128,128]{3,2,1,0:T(8,128)(2,1)} %bitcast.16, bf16[128,128,256]{2,1,0:T(8,128)(2,1)} %bitcast.14), custom_call_target="tpu_custom_call" | custom-call | tf_op jit(solution)/shard_map/forward/pallas_call | solution.py:414
  64.6 82.5 %middle.1 = (bf16[8,1024,256]{2,1,0:T(8,128)(2,1)}, bf16[1024,256]{1,0:T(8,128)(2,1)}, f32[1024,256]{1,0:T(8,128)}, f32[1024,256]{1,0:T(8,128)}) custom-call(bf16[8,1024,256]{2,1,0:T(8,128)(2,1)} %bitcast.18, bf16[1024,256]{1,0:T(8,128)(2,1)} %nodes.3, bf16[1024,256]{1,0:T(8,128)(2,1)} %cot.1, bf16[512,256]{1,0:T(8,128)(2,1)} %w_in.1, f32[1,256]{1,0:T(1,128)} %bitcast.23, ...), custom_call_target="tpu_custom_call" | custom-call | tf_op jit(solution)/shard_map/middle/pallas_call | solution.py:512
  147.2 39.7 %backward.1 = (bf16[64,4,128,128]{3,2,1,0:T(8,128)(2,1)}, bf16[128,128,256]{2,1,0:T(8,128)(2,1)}) custom-call(s32[64,4]{1,0:T(8,128)} %clamp_bitcast_fusion.cols, s32[64]{0:T(128)} %bitcast.22, bf16[64,4,128,128]{3,2,1,0:T(8,128)(2,1)} %bitcast.17, bf16[128,128,256]{2,1,0:T(8,128)(2,1)} %bitcast.15, bf16[8192,256]{1,0:T(8,128)(2,1)} %bitcast.20), custom_call_target="tpu_custom_call" | custom-call | tf_op jit(solution)/shard_map/backward/pallas_call | solution.py:577
  186.9 0.0 copy-start
  186.9 59.7 %finish.1 = (bf16[1024,256]{1,0:T(8,128)(2,1)}, f32[512,256]{1,0:T(8,128)}, f32[256,256]{1,0:T(8,128)}, f32[3,256]{1,0:T(4,128)}) custom-call(bf16[16,1024,256]{2,1,0:T(8,128)(2,1)} %bitcast.19, f32[1024,256]{1,0:T(8,128)} %get-tuple-element.19.direct, f32[1024,256]{1,0:T(8,128)} %get-tuple-element.20.weights), custom_call_target="tpu_custom_call" | custom-call | tf_op jit(solution)/shard_map/finish/pallas_call | solution.py:670
  246.6 0.0 copy-done
  246.6 0.8 copy.23
  247.4 1.9 copy.24
  249.2 1.9 copy.25
  251.1 1.7 copy.26
  252.8 1.3 copy.27
Async XLA Ops:
  186.9 59.7 %copy-start = (bf16[1024,256]{1,0:T(8,128)(2,1)S(1)}, bf16[1024,256]{1,0:T(8,128)(2,1)}, u32[]{:S(2)}) copy-start(bf16[1024,256]{1,0:T(8,128)(2,1)} %get-tuple-element.38) | copy-start | bytes 1572868

commit v3 on v2

--- a/solution.py
+++ b/solution.py
@@ -119,34 +119,38 @@
 MOVES = {"p": (3, 0, 0), "m": (1, 0, 0), "pair": (0, 1, 0), "sib": (0, 0, 1)}
 
 
-def gather(wire, group, buf, tag, src=None):
-    rows = buf.shape[1]
-    half_rows = rows // 2
-    cut = (pl.ds(0, half_rows), pl.ds(half_rows, half_rows))
+def gather(wire, group, buf, tag, per=1):
+    half_rows = buf.shape[1] // 2
+
+    def view(slot, half):
+        if per == 1:
+            return buf.at[slot, pl.ds(half * half_rows, half_rows)]
+        return buf.at[pl.ds(slot * per + half * (per // 2), per // 2)]
+
     has_sib = "sib" in group.peers
 
-    def send(ring, pair, half, way, origin=None):
-        ref = buf.at[group.slot(ring, pair), cut[half]]
+    def send(ring, pair, half, way):
+        ref = view(group.slot(ring, pair), half)
         dr, dp, dk = MOVES[way]
         name = (tag, (ring + dr) % 4, (pair + dp) % 2, dk, half)
-        wire.push(name, ref if origin is None else origin.at[cut[half]], ref, group.peers[way])
+        wire.push(name, ref, ref, group.peers[way])
 
     def take(ring, pair, half, sib=0):
         slot = group.slot(ring, pair, 1) if sib else group.slot(ring, pair)
-        wire.take((tag, ring, pair, sib, half), buf.at[slot, cut[half]], group.peers["p"])
-
-    def share(ring, pair, half, origin=None):
+        wire.take((tag, ring, pair, sib, half), view(slot, half), group.peers["p"])
+
+    def share(ring, pair, half):
         if has_sib:
-            send(ring, pair, half, "sib", origin)
-
-    send(0, 0, 0, "p", src)
-    send(0, 0, 1, "m", src)
-    send(0, 0, 0, "pair", src)
-    send(0, 0, 1, "p", src)
-    send(0, 0, 0, "m", src)
-    send(0, 0, 1, "pair", src)
+            send(ring, pair, half, "sib")
+
+    send(0, 0, 0, "p")
+    send(0, 0, 1, "m")
+    send(0, 0, 0, "pair")
+    send(0, 0, 1, "p")
+    send(0, 0, 0, "m")
+    send(0, 0, 1, "pair")
     for half in (0, 1):
-        share(0, 0, half, src)
+        share(0, 0, half)
     yield
     take(3, 0, 0)
     send(3, 0, 0, "p")
@@ -354,113 +358,112 @@
     )
 
 
-def node_gather_kernel(nodes, out, send, recv, own_sem):
-    group = RowGroup(Place())
-    greet(list(group.peers.values()))
-    own = pltpu.make_async_copy(nodes, out.at[group.slot(0, 0)], own_sem)
-    own.start()
-    wire = Wire(send, recv)
-    run(gather(wire, group, out, "n", nodes))
-    wire.drain()
-    own.wait()
-
-
-def node_gather(nodes):
-    rows, width = nodes.shape
-    return pl.pallas_call(
-        node_gather_kernel,
-        out_shape=jax.ShapeDtypeStruct((16, rows, width), BF16),
-        in_specs=[ANY],
-        out_specs=ANY,
-        scratch_shapes=[
-            pltpu.SemaphoreType.DMA((30,)),
-            pltpu.SemaphoreType.DMA((30,)),
-            pltpu.SemaphoreType.DMA,
-        ],
-        compiler_params=remote_params(1),
-        name="node_gather",
-    )(nodes)
-
-
-def forward_kernel(cols, count, tiles, nodes, out):
-    step = pl.program_id(0)
-    per = tiles.shape[0]
-    for i in range(per):
-        at = step * per + i
-        live = count[at]
-        base = pl.ds(i * 128, 128)
-
-        @pl.when(live <= 2)
-        def _():
-            pair = jnp.concatenate(
-                [jnp.where(k < live, tiles[i, k], jnp.zeros((), BF16)) for k in (0, 1)], axis=1
-            )
-            picked = jnp.concatenate([nodes[cols[at, k]] for k in (0, 1)], axis=0)
-            out[base] = dot(pair, picked).astype(BF16)
-
-        @pl.when(live > 2)
-        def _():
-            four = jnp.concatenate(
-                [jnp.where(k < live, tiles[i, k], jnp.zeros((), BF16)) for k in range(4)], axis=1
-            )
-            picked = jnp.concatenate([nodes[cols[at, k]] for k in range(4)], axis=0)
-            out[base] = dot(four, picked).astype(BF16)
-
-
-def forward(cols, count, tiles, nodes):
-    row_blocks = tiles.shape[0]
-    width = nodes.shape[-1]
-    per = 8
-    return pl.pallas_call(
-        forward_kernel,
-        out_shape=jax.ShapeDtypeStruct((row_blocks * 128, width), BF16),
-        grid_spec=pltpu.PrefetchScalarGridSpec(
-            num_scalar_prefetch=2,
-            grid=(row_blocks // per,),
-            in_specs=[
-                pl.BlockSpec((per, 4, 128, 128), lambda s, *_: (s, 0, 0, 0)),
-                pl.BlockSpec(nodes.shape, lambda s, *_: (0, 0, 0)),
-            ],
-            out_specs=pl.BlockSpec((per * 128, width), lambda s, *_: (s, 0)),
-        ),
-        compiler_params=pltpu.CompilerParams(vmem_limit_bytes=VMEM_LIMIT),
-        name="forward",
-    )(cols, count, tiles, nodes)
+ORDER = [(2, 1), (2, 0), (1, 1), (3, 1), (1, 0), (3, 0), (0, 1), (0, 0)]
 
 
 def middle_kernel(
-    partial, nodes, cot, w_in, bias, w_out, gain, shift,
-    grads, updated, direct, weights,
-    terms, relay_m, relay_p, from_m, from_p, from_pair,
-    msg_s, act_s, gproj_s, gpre_s, send, recv, load,
+    cols, live, tiles, nodes_any, nodes, cot, w_in, bias, w_out, gain, shift,
+    near0, near1, grads, updated, direct, gw_in, gw_out, gvec,
+    slots, terms0, terms1, *rest,
 ):
-    group = ColGroup(Place())
+    bufs0, bufs1, rest = rest[:5], rest[5:10], rest[10:]
+    msg_s, act_s, gproj_s, gpre_s, weights = rest[:5]
+    sum_bufs, (send, recv, load) = rest[5:10], rest[10:]
+    place = Place()
+    across, along = RowGroup(place), ColGroup(place)
     width = nodes.shape[1]
     rows = nodes.shape[0]
+    near, terms = (near0, near1), (terms0, terms1)
+
+    mine = [
+        pltpu.make_async_copy(
+            nodes_any.at[:, :, pl.ds(h * 128, 128)],
+            near[h].at[pl.ds(across.slot(0, 0) * 8, 8)],
+            load.at[8 + h],
+        )
+        for h in (0, 1)
+    ]
+    for copy in mine:
+        copy.start()
 
     def loader(ring, pair):
-        slot = group.slot(ring, pair)
-        return pltpu.make_async_copy(partial.at[slot], terms.at[slot], load.at[ring * 2 + pair])
-
-    for ring in (2, 1, 3, 0):
-        for pair in (1, 0):
-            loader(ring, pair).start()
-    greet(list(group.peers.values()))
+        at = pl.ds(along.slot(ring, pair) * 8, 8)
+        return pltpu.make_async_copy(tiles.at[at], slots.at[at], load.at[ring * 2 + pair])
+
+    for at in ORDER:
+        loader(*at).start()
+    greet(place.all_peers())
     wire = Wire(send, recv)
-    bufs = (relay_m, relay_p, from_m, from_p, from_pair)
-    run(scatter(wire, group, terms, bufs, "s", lambda ring, pair: loader(ring, pair).wait()))
-    own = group.slot(0, 0)
-    gvec = weights.at[pl.ds(3 * width, 8)]
+    for copy in mine:
+        copy.wait()
+
+    def mask(ring, pair):
+        loader(ring, pair).wait()
+        base = along.slot(ring, pair) * 8
+
+        def one(i, carry):
+            for k in range(4):
+                keep = live[base + i, pl.ds(k, 1)].astype(BF16)
+                slots[base + i, k] = slots[base + i, k] * keep
+            return carry
+
+        lax.fori_loop(0, 8, one, 0)
+
+    def product(h, ring, pair):
+        slot = along.slot(ring, pair)
+
+        def one(j, carry):
+            for u in range(2):
+                i = slot * 8 + j * 2 + u
+                left = jnp.concatenate([slots[i, k] for k in range(4)], axis=1)
+                right = []
+                for k in range(4):
+                    right.append(near[h][cols[i, k]])
+                at = pl.ds(pl.multiple_of((j * 2 + u) * 128, 128), 128)
+                terms[h][slot, at] = dot(left, jnp.concatenate(right, axis=0)).astype(BF16)
+            return carry
+
+        lax.fori_loop(0, 4, one, 0)
+
+    gather0 = gather(wire, across, near0, "n0", 8)
+    gather1 = gather(wire, across, near1, "n1", 8)
+    for step in range(5):
+        next(gather0)
+        for at in ORDER[2 * step : 2 * step + 2]:
+            mask(*at)
+    next(gather1)
+    run(gather0)
+
+    def prepare0(ring, pair):
+        product(0, ring, pair)
+        next(gather1, None)
+
+    scatter0 = scatter(wire, along, terms0, bufs0, "s0", prepare0)
+    for _ in range(4):
+        next(scatter0)
+    run(gather1)
+    scatter1 = scatter(wire, along, terms1, bufs1, "s1", lambda *at: product(1, *at))
+    for _ in scatter1:
+        next(scatter0, None)
+    run(scatter0)
+    own = along.slot(0, 0)
+    gsum = weights.at[pl.ds(3 * width, 8)]
     weights[3 * width :] = jnp.zeros((weights.shape[0] - 3 * width, width), F32)
 
     def chunk(i, carry):
         at = pl.ds(pl.multiple_of(i * 256, 256), 256)
-        msg = (
-            terms[own, at].astype(F32)
-            + from_m[0, at].astype(F32)
-            + from_p[0, at].astype(F32)
-            + from_pair[at].astype(F32)
-        ).astype(BF16)
+        msg = jnp.concatenate(
+            [
+                (
+                    terms[h][own, at].astype(F32)
+                    + bufs[2][0, at].astype(F32)
+                    + bufs[3][0, at].astype(F32)
+                    + bufs[4][at].astype(F32)
+                ).astype(BF16)
+                for h, bufs in ((0, bufs0), (1, bufs1))
+            ],
+            axis=1,
+        )
         msg_s[at] = msg
         mine = nodes[at]
         pre = dot(mine, w_in[:width]) + dot(msg, w_in[width:]) + bias[...]
@@ -491,48 +494,66 @@
         gpre_s[at] = gpre_b
         grads[own, at] = dot(gpre_b, w_in[width:], ((1,), (1,))).astype(BF16)
         direct[at] = grad_out + dot(gpre_b, w_in[:width], ((1,), (1,)))
-        gvec[0:1] += jnp.sum(gpre, axis=0, keepdims=True)
-        gvec[1:2] += jnp.sum(grad_out * normed, axis=0, keepdims=True)
-        gvec[2:3] += jnp.sum(grad_out, axis=0, keepdims=True)
+        gsum[0:1] += jnp.sum(gpre, axis=0, keepdims=True)
+        gsum[1:2] += jnp.sum(grad_out * normed, axis=0, keepdims=True)
+        gsum[2:3] += jnp.sum(grad_out, axis=0, keepdims=True)
         return carry
 
     lax.fori_loop(0, rows // 256, chunk, 0)
-    steps = gather(wire, group, grads, "g")
+    steps = gather(wire, along, grads, "g")
     next(steps)
     weights[:width] = dot(nodes[...], gpre_s[...], ((0,), (0,)))
     weights[width : 2 * width] = dot(msg_s[...], gpre_s[...], ((0,), (0,)))
     weights[2 * width : 3 * width] = dot(act_s[...], gproj_s[...], ((0,), (0,)))
-    run(steps)
+    sums = total(wire, place, weights, sum_bufs, "w")
+    next(sums)
+    for _ in steps:
+        next(sums, None)
+    run(sums)
+    result = sum_bufs[0]
+    factor = F32(131072.0) ** F32(-0.5)
+    gw_in[...] = result[: 2 * width] * factor
+    gw_out[...] = result[2 * width : 3 * width] * factor
+    gvec[...] = result[3 * width : 3 * width + 3] * factor
     wire.drain()
 
 
-def middle(partial, nodes, cot, w_in, bias, w_out, gain, shift):
+def middle(cols, live, tiles, nodes, cot, w_in, bias, w_out, gain, shift):
     rows, width = nodes.shape
     one = functools.partial(pltpu.VMEM, (rows, width))
+    smem = pl.BlockSpec(memory_space=pltpu.SMEM)
+    near = jax.ShapeDtypeStruct((128, 128, 128), BF16)
     return pl.pallas_call(
         middle_kernel,
         out_shape=[
+            near,
+            near,
             jax.ShapeDtypeStruct((8, rows, width), BF16),
             jax.ShapeDtypeStruct((rows, width), BF16),
             jax.ShapeDtypeStruct((rows, width), F32),
-            jax.ShapeDtypeStruct((TOTAL_ROWS, width), F32),
+            jax.ShapeDtypeStruct((2 * width, width), F32),
+            jax.ShapeDtypeStruct((width, width), F32),
+            jax.ShapeDtypeStruct((3, width), F32),
         ],
-        in_specs=[ANY] + [VM] * 7,
-        out_specs=[VM] * 4,
-        scratch_shapes=[pltpu.VMEM((8, rows, width), BF16)]
-        + scatter_shapes(rows, width)
+        in_specs=[smem, VM, ANY, ANY] + [VM] * 7,
+        out_specs=[VM] * 8,
+        scratch_shapes=[pltpu.VMEM(tiles.shape, BF16)]
+        + [pltpu.VMEM((8, rows, 128), BF16)] * 2
+        + scatter_shapes(rows, 128) * 2
         + [one(BF16)] * 4
+        + [pltpu.VMEM((TOTAL_ROWS, width), F32)]
+        + total_shapes(width)
         + [
-            pltpu.SemaphoreType.DMA((40,)),
-            pltpu.SemaphoreType.DMA((40,)),
-            pltpu.SemaphoreType.DMA((8,)),
+            pltpu.SemaphoreType.DMA((140,)),
+            pltpu.SemaphoreType.DMA((140,)),
+            pltpu.SemaphoreType.DMA((10,)),
         ],
         compiler_params=remote_params(2),
         name="middle",
-    )(partial.reshape(8, rows, width), nodes, cot, w_in, bias, w_out, gain, shift)
-
-
-def backward_kernel(cols, count, tiles, nodes, grads, tile_grads, back, acc):
+    )(cols, live, tiles, nodes.reshape(8, 128, width), nodes, cot, w_in, bias, w_out, gain, shift)
+
+
+def backward_kernel(cols, count, tiles, near0, near1, grads, tile_grads, back, acc):
     step = pl.program_id(0)
     per = tiles.shape[0]
 
@@ -554,7 +575,8 @@
             def _():
                 col = cols[at, k]
                 grad = grads[base]
-                tile_grads[i, k] = (dot(grad, nodes[col], ((1,), (1,))) * scale).astype(BF16)
+                picked = jnp.concatenate([near0[col], near1[col]], axis=1)
+                tile_grads[i, k] = (dot(grad, picked, ((1,), (1,))) * scale).astype(BF16)
                 acc[col] += dot(tiles[i, k], grad, ((0,), (0,)))
 
             @pl.when(k >= live)
@@ -570,59 +592,54 @@
         lax.fori_loop(0, acc.shape[0], put, 0)
 
 
-def backward(cols, count, tiles, nodes, grads):
+def backward(cols, count, tiles, near0, near1, grads):
     row_blocks = tiles.shape[0]
-    blocks, _, width = nodes.shape
+    width = grads.shape[1]
+    columns = (128, 128, width)
+    near = pl.BlockSpec(near0.shape, lambda s, *_: (0, 0, 0), pipeline_mode=pl.Buffered(1))
     per = 8
     return pl.pallas_call(
         backward_kernel,
         out_shape=[
             jax.ShapeDtypeStruct(tiles.shape, BF16),
-            jax.ShapeDtypeStruct(nodes.shape, BF16),
+            jax.ShapeDtypeStruct(columns, BF16),
         ],
         grid_spec=pltpu.PrefetchScalarGridSpec(
             num_scalar_prefetch=2,
             grid=(row_blocks // per,),
             in_specs=[
                 pl.BlockSpec((per, 4, 128, 128), lambda s, *_: (s, 0, 0, 0)),
-                pl.BlockSpec(nodes.shape, lambda s, *_: (0, 0, 0), pipeline_mode=pl.Buffered(1)),
+                near,
+                near,
                 pl.BlockSpec((per * 128, width), lambda s, *_: (s, 0)),
             ],
             out_specs=[
                 pl.BlockSpec((per, 4, 128, 128), lambda s, *_: (s, 0, 0, 0)),
-                pl.BlockSpec(nodes.shape, lambda s, *_: (0, 0, 0), pipeline_mode=pl.Buffered(1)),
+                pl.BlockSpec(columns, lambda s, *_: (0, 0, 0), pipeline_mode=pl.Buffered(1)),
             ],
-            scratch_shapes=[pltpu.VMEM(nodes.shape, F32)],
+            scratch_shapes=[pltpu.VMEM(columns, F32)],
         ),
         compiler_params=pltpu.CompilerParams(vmem_limit_bytes=VMEM_LIMIT),
         name="backward",
-    )(cols, count, tiles, nodes, grads)
+    )(cols, count, tiles, near0, near1, grads)
 
 
 def finish_kernel(
-    back, direct, weights, out, gw_in, gw_out, gvec,
-    terms, others, relay_m, relay_p, from_m, from_p, from_pair,
-    mine, result, in_core, in_x, in_y, in_z, send, recv, load,
+    back, direct, out,
+    terms, others, relay_m, relay_p, from_m, from_p, from_pair, send, recv, load,
 ):
-    place = Place()
-    group = RowGroup(place)
+    group = RowGroup(Place())
     rows = terms.shape[1]
-    order = [(2, 1), (2, 0), (1, 1), (3, 1), (1, 0), (3, 0), (0, 1), (0, 0)]
 
     def loader(ring, pair):
         slot = group.slot(ring, pair)
         return pltpu.make_async_copy(back.at[slot], terms.at[slot], load.at[ring * 2 + pair])
 
-    whole = pltpu.make_async_copy(weights, mine, load.at[8])
-    whole.start()
-    for at in order:
+    for at in ORDER:
         loader(*at).start()
-    greet(place.all_peers())
+    greet(list(group.peers.values()))
     wire = Wire(send, recv)
-    whole.wait()
-    sums = total(wire, place, mine, (result, in_core, in_x, in_y, in_z), "w")
-    next(sums)
-    for ring, pair in order:
+    for ring, pair in ORDER:
         wire.push(
             ("f", ring, pair),
             back.at[group.slot(ring, pair, 1)],
@@ -642,8 +659,7 @@
         add_rows(rows, 128, body)
 
     bufs = (relay_m, relay_p, from_m, from_p, from_pair)
-    for _ in scatter(wire, group, terms, bufs, "b", prepare):
-        next(sums, None)
+    run(scatter(wire, group, terms, bufs, "b", prepare))
     own = group.slot(0, 0)
 
     def last(at):
@@ -656,34 +672,21 @@
         ).astype(BF16)
 
     add_rows(rows, 128, last)
-    run(sums)
-    width = out.shape[1]
-    factor = F32(131072.0) ** F32(-0.5)
-    gw_in[...] = result[: 2 * width] * factor
-    gw_out[...] = result[2 * width : 3 * width] * factor
-    gvec[...] = result[3 * width : 3 * width + 3] * factor
     wire.drain()
 
 
-def finish(back, direct, weights):
+def finish(back, direct):
     rows, width = direct.shape
     return pl.pallas_call(
         finish_kernel,
-        out_shape=[
-            jax.ShapeDtypeStruct((rows, width), BF16),
-            jax.ShapeDtypeStruct((2 * width, width), F32),
-            jax.ShapeDtypeStruct((width, width), F32),
-            jax.ShapeDtypeStruct((3, width), F32),
-        ],
-        in_specs=[ANY, VM, ANY],
-        out_specs=[VM] * 4,
+        out_shape=jax.ShapeDtypeStruct((rows, width), BF16),
+        in_specs=[ANY, VM],
+        out_specs=VM,
         scratch_shapes=[
             pltpu.VMEM((16, rows, width), BF16),
             pltpu.VMEM((8, rows, width), BF16),
         ]
         + scatter_shapes(rows, width)
-        + [pltpu.VMEM((TOTAL_ROWS, width), F32)]
-        + total_shapes(width)
         + [
             pltpu.SemaphoreType.DMA((60,)),
             pltpu.SemaphoreType.DMA((60,)),
@@ -691,7 +694,7 @@
         ],
         compiler_params=remote_params(3),
         name="finish",
-    )(back.reshape(16, rows, width), direct, weights)
+    )(back.reshape(16, rows, width), direct)
 
 
 def body(nodes, tiles, tile_col, tile_count, w_in, bias_in, w_out, ln_gain, ln_shift, cotangent):
@@ -699,13 +702,13 @@
     cols, count = tile_col[:, 0], tile_count[:, 0]
     slots = tiles[:, 0]
     cols = jnp.clip(cols, 0, 127)
-    gathered = node_gather(nodes).reshape(128, 128, width)
-    partial = forward(cols, count, slots, gathered)
-    grads, updated, direct, weights = middle(
-        partial, nodes, cotangent, w_in, bias_in[None], w_out, ln_gain[None], ln_shift[None]
+    live = lax.broadcasted_iota(jnp.int32, (64, 4, 128), 1) < count[:, None, None]
+    live = live.astype(F32)
+    near0, near1, grads, updated, direct, gw_in, gw_out, gvec = middle(
+        cols, live, slots, nodes, cotangent, w_in, bias_in[None], w_out, ln_gain[None], ln_shift[None]
     )
-    grad_tiles, back = backward(cols, count, slots, gathered, grads.reshape(8 * rows, width))
-    grad_nodes, gw_in, gw_out, gvec = finish(back, direct, weights)
+    grad_tiles, back = backward(cols, count, slots, near0, near1, grads.reshape(8 * rows, width))
+    grad_nodes = finish(back, direct)
     return updated, grad_nodes, grad_tiles[:, None], gw_in, gw_out, gvec
 
 

time: 257 us -> 231 us (0.90)
  Pallas kernels: 245 us -> 221 us
  local copies, waits for them, and re-layouts: 8.25 us -> 5.54 us
    pallas_call x4 -> x2, Pallas kernels: 205 us -> 182 us  [the longest x1 133 us: middle(): pl.pallas_call(middle_kernel, out_shape=[near, near, jax.ShapeDtypeStruct...]
    unnamed x8 -> x14, local copies, waits for them, and re-layouts: 8.25 us -> 5.54 us
where the time goes in v3:
time: 231 us; the launch traced here: 229 us
  Pallas kernels  221 us (96%)
  local copies, waits for them, and re-layouts  5.54 us (2%)
    pallas_call x1, Pallas kernels, middle(): pl.pallas_call(middle_kernel, out_shape=[near, near, jax.ShapeDtypeStruct...  133 us
    pallas_call x1, Pallas kernels, finish(): pl.pallas_call(finish_kernel, out_shape=jax.ShapeDtypeStruct((rows, width...  48.5 us
    pallas_call x1, Pallas kernels, backward(): pl.pallas_call(backward_kernel, out_shape=[jax.ShapeDtypeStruct(tiles.sha...  38.6 us
    unnamed x14, local copies, waits for them, and re-layouts  5.54 us

profile of v3, /device:TPU:1, one launch (start us, length us, event | category | flops | bytes accessed | tf_op | source)
XLA Modules:
  0.0 228.8 jit_solution(4354524504083100407)
XLA Ops:
  0.6 0.8 copy.16
  1.4 0.6 clamp_bitcast_fusion.cols
  2.0 1.4 fusion.live
  3.5 133.4 %middle.1 = (bf16[128,128,128]{2,1,0:T(8,128)(2,1)}, bf16[128,128,128]{2,1,0:T(8,128)(2,1)}, bf16[8,1024,256]{2,1,0:T(8,128)(2,1)}, bf16[1024,256]{1,0:T(8,128)(...) custom-call(s32[64,4]{1,0:T(8,128)} %clamp_bitcast_fusion.cols, ...), custom_call_target="tpu_custom_call" | custom-call | tf_op jit(solution)/shard_map/middle/pallas_call | solution.py:526
  136.9 38.6 %backward.1 = (bf16[64,4,128,128]{3,2,1,0:T(8,128)(2,1)}, bf16[128,128,256]{2,1,0:T(8,128)(2,1)}) custom-call(s32[64,4]{1,0:T(8,128)} %clamp_bitcast_fusion.cols, s32[64]{0:T(128)} %bitcast.19, bf16[64,4,128,128]{3,2,1,0:T(8,128)(2,1)} %bitcast.14, bf16[128,128,128]{2,1,0:T(8,128)(2,1)} %get-tuple-element.17.near0, ...), custom_call_target="tpu_custom_call" | custom-call | tf_op jit(solution)/shard_map/backward/pallas_call | solution.py:601
  175.5 0.0 copy-start.1
  175.5 0.0 copy-start
  175.5 0.0 copy-start.2
  175.5 0.0 copy-start.3
  175.5 48.5 %finish.1 = bf16[1024,256]{1,0:T(8,128)(2,1)} custom-call(bf16[16,1024,256]{2,1,0:T(8,128)(2,1)} %bitcast.15, f32[1024,256]{1,0:T(8,128)} %get-tuple-element.21.direct), custom_call_target="tpu_custom_call" | custom-call | tf_op jit(solution)/shard_map/finish/pallas_call | solution.py:680
  224.1 0.0 copy-done.1
  224.1 0.8 copy.23
  224.9 1.9 copy.24
  226.7 0.0 copy-done
  226.8 0.8 copy.25
  227.5 0.0 copy-done.2
  227.5 0.7 copy.26
  228.2 0.0 copy-done.3
  228.3 0.6 copy.27
Async XLA Ops:
  175.5 48.6 %copy-start.1 = (bf16[1024,256]{1,0:T(8,128)(2,1)S(1)}, bf16[1024,256]{1,0:T(8,128)(2,1)}, u32[]{:S(2)}) copy-start(bf16[1024,256]{1,0:T(8,128)(2,1)} %get-tuple-element.38) | copy-start | bytes 1572868
  175.5 51.3 %copy-start = (f32[512,256]{1,0:T(8,128)S(1)}, f32[512,256]{1,0:T(8,128)}, u32[]{:S(2)}) copy-start(f32[512,256]{1,0:T(8,128)} %get-tuple-element.41) | copy-start | bytes 1572868
  175.5 52.0 %copy-start.2 = (f32[256,256]{1,0:T(8,128)S(1)}, f32[256,256]{1,0:T(8,128)}, u32[]{:S(2)}) copy-start(f32[256,256]{1,0:T(8,128)} %get-tuple-element.42) | copy-start | bytes 786436
  175.5 52.7 %copy-start.3 = (f32[3,256]{1,0:T(4,128)S(1)}, f32[3,256]{1,0:T(4,128)}, u32[]{:S(2)}) copy-start(f32[3,256]{1,0:T(4,128)} %get-tuple-element.43) | copy-start | bytes 9220

commit v4 on v3

--- a/solution.py
+++ b/solution.py
@@ -363,8 +363,8 @@
 
 def middle_kernel(
     cols, live, tiles, nodes_any, nodes, cot, w_in, bias, w_out, gain, shift,
-    near0, near1, grads, updated, direct, gw_in, gw_out, gvec,
-    slots, terms0, terms1, *rest,
+    near0_out, near1_out, grads, updated, direct, gw_in, gw_out, gvec,
+    near0, near1, slots, terms0, terms1, *rest,
 ):
     bufs0, bufs1, rest = rest[:5], rest[5:10], rest[10:]
     msg_s, act_s, gproj_s, gpre_s, weights = rest[:5]
@@ -442,6 +442,12 @@
     for _ in range(4):
         next(scatter0)
     run(gather1)
+    leaving = [
+        pltpu.make_async_copy(near[h], out, load.at[10 + h])
+        for h, out in ((0, near0_out), (1, near1_out))
+    ]
+    for copy in leaving:
+        copy.start()
     scatter1 = scatter(wire, along, terms1, bufs1, "s1", lambda *at: product(1, *at))
     for _ in scatter1:
         next(scatter0, None)
@@ -515,6 +521,8 @@
     gw_in[...] = result[: 2 * width] * factor
     gw_out[...] = result[2 * width : 3 * width] * factor
     gvec[...] = result[3 * width : 3 * width + 3] * factor
+    for copy in leaving:
+        copy.wait()
     wire.drain()
 
 
@@ -536,8 +544,9 @@
             jax.ShapeDtypeStruct((3, width), F32),
         ],
         in_specs=[smem, VM, ANY, ANY] + [VM] * 7,
-        out_specs=[VM] * 8,
-        scratch_shapes=[pltpu.VMEM(tiles.shape, BF16)]
+        out_specs=[ANY] * 2 + [VM] * 6,
+        scratch_shapes=[pltpu.VMEM((128, 128, 128), BF16)] * 2
+        + [pltpu.VMEM(tiles.shape, BF16)]
         + [pltpu.VMEM((8, rows, 128), BF16)] * 2
         + scatter_shapes(rows, 128) * 2
         + [one(BF16)] * 4
@@ -546,16 +555,23 @@
         + [
             pltpu.SemaphoreType.DMA((140,)),
             pltpu.SemaphoreType.DMA((140,)),
-            pltpu.SemaphoreType.DMA((10,)),
+            pltpu.SemaphoreType.DMA((12,)),
         ],
         compiler_params=remote_params(2),
         name="middle",
     )(cols, live, tiles, nodes.reshape(8, 128, width), nodes, cot, w_in, bias, w_out, gain, shift)
 
 
-def backward_kernel(cols, count, tiles, near0, near1, grads, tile_grads, back, acc):
+def backward_kernel(
+    cols, count, tiles, near0, near1, grads, updated_in, gw_in_in, gw_out_in, gvec_in,
+    tile_grads, back, updated, gw_in, gw_out, gvec, acc,
+):
     step = pl.program_id(0)
     per = tiles.shape[0]
+    updated[...] = updated_in[...]
+    gw_in[...] = gw_in_in[...]
+    gw_out[...] = gw_out_in[...]
+    gvec[...] = gvec_in[...]
 
     @pl.when(step == 0)
     def _():
@@ -566,22 +582,47 @@
         lax.fori_loop(0, acc.shape[0], clear, 0)
 
     scale = F32(256.0) ** F32(-0.5)
-    for i in range(per):
-        at = step * per + i
+
+    def work(i, at, slots):
         live = count[at]
-        base = pl.ds(i * 128, 128)
-        for k in range(4):
-            @pl.when(k < live)
-            def _():
-                col = cols[at, k]
-                grad = grads[base]
-                picked = jnp.concatenate([near0[col], near1[col]], axis=1)
-                tile_grads[i, k] = (dot(grad, picked, ((1,), (1,))) * scale).astype(BF16)
-                acc[col] += dot(tiles[i, k], grad, ((0,), (0,)))
-
-            @pl.when(k >= live)
-            def _():
-                tile_grads[i, k] = jnp.zeros((128, 128), BF16)
+        grad = grads[pl.ds(i * 128, 128)]
+        which = [cols[at, k] for k in range(slots)]
+        picked = jnp.concatenate(
+            [jnp.concatenate([near0[c], near1[c]], axis=1) for c in which], axis=0
+        )
+        made = (dot(grad, picked, ((1,), (1,))) * scale).astype(BF16)
+        zero = jnp.zeros((128, 128), BF16)
+        for k in range(slots):
+            tile_grads[i, k] = jnp.where(k < live, made[:, k * 128 : k * 128 + 128], zero)
+        kept = jnp.concatenate([jnp.where(k < live, tiles[i, k], zero) for k in range(slots)], axis=1)
+        return which, dot(kept, grad, ((0,), (0,)))
+
+    def both(i, slots):
+        found = [work(i + u, step * per + i + u, slots) for u in (0, 1)]
+        for which, terms in found:
+            for k in range(slots):
+                acc[which[k]] += terms[k * 128 : k * 128 + 128]
+
+    for i in range(0, per, 2):
+        most = jnp.maximum(count[step * per + i], count[step * per + i + 1])
+
+        @pl.when(most <= 2)
+        def _():
+            for u in (0, 1):
+                tile_grads[i + u, 2:4] = jnp.zeros((2, 128, 128), BF16)
+
+        @pl.when(most <= 0)
+        def _():
+            for u in (0, 1):
+                tile_grads[i + u, 0:2] = jnp.zeros((2, 128, 128), BF16)
+
+        @pl.when((most > 0) & (most <= 2))
+        def _():
+            both(i, 2)
+
+        @pl.when(most > 2)
+        def _():
+            both(i, 4)
 
     @pl.when(step == pl.num_programs(0) - 1)
     def _():
@@ -592,36 +633,45 @@
         lax.fori_loop(0, acc.shape[0], put, 0)
 
 
-def backward(cols, count, tiles, near0, near1, grads):
+def backward(cols, count, tiles, near0, near1, grads, updated, gw_in, gw_out, gvec):
     row_blocks = tiles.shape[0]
     width = grads.shape[1]
     columns = (128, 128, width)
     near = pl.BlockSpec(near0.shape, lambda s, *_: (0, 0, 0), pipeline_mode=pl.Buffered(1))
     per = 8
+    steps = row_blocks // per
+
+    def cut(array):
+        return pl.BlockSpec((array.shape[0] // steps, width), lambda s, *_: (s, 0))
+
+    passed = [cut(updated), cut(gw_in), cut(gw_out), pl.BlockSpec((3, width), lambda s, *_: (0, 0))]
     return pl.pallas_call(
         backward_kernel,
         out_shape=[
             jax.ShapeDtypeStruct(tiles.shape, BF16),
             jax.ShapeDtypeStruct(columns, BF16),
-        ],
+        ]
+        + [jax.ShapeDtypeStruct(a.shape, a.dtype) for a in (updated, gw_in, gw_out, gvec)],
         grid_spec=pltpu.PrefetchScalarGridSpec(
             num_scalar_prefetch=2,
-            grid=(row_blocks // per,),
+            grid=(steps,),
             in_specs=[
                 pl.BlockSpec((per, 4, 128, 128), lambda s, *_: (s, 0, 0, 0)),
                 near,
                 near,
                 pl.BlockSpec((per * 128, width), lambda s, *_: (s, 0)),
-            ],
+            ]
+            + passed,
             out_specs=[
                 pl.BlockSpec((per, 4, 128, 128), lambda s, *_: (s, 0, 0, 0)),
                 pl.BlockSpec(columns, lambda s, *_: (0, 0, 0), pipeline_mode=pl.Buffered(1)),
-            ],
+            ]
+            + passed,
             scratch_shapes=[pltpu.VMEM(columns, F32)],
         ),
         compiler_params=pltpu.CompilerParams(vmem_limit_bytes=VMEM_LIMIT),
         name="backward",
-    )(cols, count, tiles, near0, near1, grads)
+    )(cols, count, tiles, near0, near1, grads, updated, gw_in, gw_out, gvec)
 
 
 def finish_kernel(
@@ -707,7 +757,9 @@
     near0, near1, grads, updated, direct, gw_in, gw_out, gvec = middle(
         cols, live, slots, nodes, cotangent, w_in, bias_in[None], w_out, ln_gain[None], ln_shift[None]
     )
-    grad_tiles, back = backward(cols, count, slots, near0, near1, grads.reshape(8 * rows, width))
+    grad_tiles, back, updated, gw_in, gw_out, gvec = backward(
+        cols, count, slots, near0, near1, grads.reshape(8 * rows, width), updated, gw_in, gw_out, gvec
+    )
     grad_nodes = finish(back, direct)
     return updated, grad_nodes, grad_tiles[:, None], gw_in, gw_out, gvec
 

time: 231 us -> 206 us (0.89)
  Pallas kernels: 221 us -> 200 us
  local copies, waits for them, and re-layouts: 5.54 us -> 2.64 us
    pallas_call x1, Pallas kernels: 38.6 us -> 26 us  [backward(): pl.pallas_call(backward_kernel, out_shape=[jax.ShapeDtypeStruct(tiles.sha...]
    pallas_call x1, Pallas kernels: 48.5 us -> 43.2 us  [finish(): pl.pallas_call(finish_kernel, out_shape=jax.ShapeDtypeStruct((rows, width...]
    unnamed x14 -> x2, local copies, waits for them, and re-layouts: 5.54 us -> 2.64 us
    pallas_call x1, Pallas kernels: 133 us -> 131 us  [middle(): pl.pallas_call(middle_kernel, out_shape=[near, near, jax.ShapeDtypeStruct...]
where the time goes in v4:
time: 206 us
  Pallas kernels  200 us (97%)
  local copies, waits for them, and re-layouts  2.64 us (1%)
  other arithmetic  2.07 us (1%)
    pallas_call x1, Pallas kernels, middle(): pl.pallas_call(middle_kernel, out_shape=[near, near, jax.ShapeDtypeStruct...  131 us
    pallas_call x1, Pallas kernels, finish(): pl.pallas_call(finish_kernel, out_shape=jax.ShapeDtypeStruct((rows, width...  43.2 us
    pallas_call x1, Pallas kernels, backward(): pl.pallas_call(backward_kernel, out_shape=[jax.ShapeDtypeStruct(tiles.sha...  26 us

profile of v4, /device:TPU:1, one launch (start us, length us, event | category | flops | bytes accessed | tf_op | source)
XLA Modules:
  0.0 205.6 jit_solution(7810069167329924443)
XLA Ops:
  0.6 0.8 copy.16
  1.4 0.6 clamp_bitcast_fusion.cols
  2.0 1.4 fusion.live
  3.5 131.0 %middle.1 = (bf16[128,128,128]{2,1,0:T(8,128)(2,1)}, bf16[128,128,128]{2,1,0:T(8,128)(2,1)}, bf16[8,1024,256]{2,1,0:T(8,128)(2,1)}, bf16[1024,256]{1,0:T(8,128)(...) custom-call(s32[64,4]{1,0:T(8,128)} %clamp_bitcast_fusion.cols, ...), custom_call_target="tpu_custom_call" | custom-call | tf_op jit(solution)/shard_map/middle/pallas_call | solution.py:534
  134.5 26.0 %backward.1 = (bf16[64,4,128,128]{3,2,1,0:T(8,128)(2,1)}, bf16[128,128,256]{2,1,0:T(8,128)(2,1)}, bf16[1024,256]{1,0:T(8,128)(2,1)}, f32[512,256]{1,0:T(8,128)}, f32[256,256]{1,0:T(8,128)}, /*index=5*/f32[3,256]{1,0:T(4,128)}) custom-call(s32[64,4]{1,0:T(8,128)} %clamp_bitcast_fusion.cols, s32[64]{0:T(128)} %bitcast.19, bf16[64,4,128,128]{3,2,1,0:T(8,128)(2,1)} %bitcast.14, ...), custom_call_target="tpu_custom_call" | custom-call | tf_op jit(solution)/shard_map/backward/pallas_call | solution.py:648
  160.5 43.2 %finish.1 = bf16[1024,256]{1,0:T(8,128)(2,1)} custom-call(bf16[16,1024,256]{2,1,0:T(8,128)(2,1)} %bitcast.15, f32[1024,256]{1,0:T(8,128)} %get-tuple-element.29.direct), custom_call_target="tpu_custom_call" | custom-call | tf_op jit(solution)/shard_map/finish/pallas_call | solution.py:730
  203.7 1.9 copy.19

commit v5 on v4

--- a/solution.py
+++ b/solution.py
@@ -9,7 +9,7 @@
 
 F32, BF16 = jnp.float32, jnp.bfloat16
 MIB = 1024 * 1024
-VMEM_LIMIT = 56 * MIB
+VMEM_LIMIT = 58 * MIB
 EPS = 1e-05
 TOTAL_ROWS = 1024
 
@@ -119,81 +119,102 @@
 MOVES = {"p": (3, 0, 0), "m": (1, 0, 0), "pair": (0, 1, 0), "sib": (0, 0, 1)}
 
 
-def gather(wire, group, buf, tag, per=1):
-    half_rows = buf.shape[1] // 2
-
-    def view(slot, half):
+QUARTER = ((0, 3, False), (3, 3, False), (6, 1, True), (7, 1, True))
+MORE = ((0, 3, False), (3, 2, False), (5, 1, True), (6, 2, True))
+
+
+def gather(wire, group, buf, tag, parts, per=1):
+    unit = buf.shape[1] // 8
+
+    def view(slot, part):
+        start, size, _ = parts[part]
         if per == 1:
-            return buf.at[slot, pl.ds(half * half_rows, half_rows)]
-        return buf.at[pl.ds(slot * per + half * (per // 2), per // 2)]
+            return buf.at[slot, pl.ds(start * unit, size * unit)]
+        return buf.at[pl.ds(slot * per + start, size)]
 
     has_sib = "sib" in group.peers
-
-    def send(ring, pair, half, way):
-        ref = view(group.slot(ring, pair), half)
+    late = [c for c in range(4) if parts[c][2]]
+    early = [c for c in range(4) if not parts[c][2]]
+
+    def send(ring, pair, part, way):
+        ref = view(group.slot(ring, pair), part)
         dr, dp, dk = MOVES[way]
-        name = (tag, (ring + dr) % 4, (pair + dp) % 2, dk, half)
+        name = (tag, (ring + dr) % 4, (pair + dp) % 2, dk, part)
         wire.push(name, ref, ref, group.peers[way])
 
-    def take(ring, pair, half, sib=0):
+    def take(ring, pair, part, sib=0):
         slot = group.slot(ring, pair, 1) if sib else group.slot(ring, pair)
-        wire.take((tag, ring, pair, sib, half), view(slot, half), group.peers["p"])
-
-    def share(ring, pair, half):
+        wire.take((tag, ring, pair, sib, part), view(slot, part), group.peers["p"])
+
+    def share(ring, pair, part):
         if has_sib:
-            send(ring, pair, half, "sib")
-
-    send(0, 0, 0, "p")
-    send(0, 0, 1, "m")
-    send(0, 0, 0, "pair")
-    send(0, 0, 1, "p")
-    send(0, 0, 0, "m")
-    send(0, 0, 1, "pair")
-    for half in (0, 1):
-        share(0, 0, half)
-    yield
-    take(3, 0, 0)
-    send(3, 0, 0, "p")
-    take(1, 0, 1)
-    send(1, 0, 1, "m")
-    share(3, 0, 0)
-    share(1, 0, 1)
-    yield
-    for half in (0, 1):
-        take(0, 1, half)
-        send(0, 1, half, "p")
-        send(0, 1, half, "m")
-        share(0, 1, half)
-    yield
-    take(3, 0, 1)
-    take(1, 0, 0)
-    share(3, 0, 1)
-    share(1, 0, 0)
-    yield
-    take(3, 1, 0)
-    send(3, 1, 0, "p")
-    take(1, 1, 1)
-    send(1, 1, 1, "m")
-    share(3, 1, 0)
-    share(1, 1, 1)
-    yield
-    for half in (0, 1):
-        take(2, 0, half)
-        share(2, 0, half)
-    yield
-    take(3, 1, 1)
-    take(1, 1, 0)
-    share(3, 1, 1)
-    share(1, 1, 0)
-    for half in (0, 1):
-        take(2, 1, half)
-        share(2, 1, half)
+            send(ring, pair, part, "sib")
+
+    def relay(pair, which):
+        for c in which:
+            ring, way = ((3, "p"), (1, "m"))[c % 2]
+            take(ring, pair, c)
+            send(ring, pair, c, way)
+            if c in late and pair == 0:
+                send(ring, pair, c, "pair")
+            share(ring, pair, c)
+
+    def rest(pair, which):
+        for c in which:
+            ring = (1, 3)[c % 2]
+            take(ring, pair, c)
+            if c in late and pair == 0:
+                send(ring, pair, c, "pair")
+            share(ring, pair, c)
+
+    for c in early:
+        send(0, 0, c, "pair")
+    for c in early + late:
+        send(0, 0, c, ("p", "m")[c % 2])
+    for c in early + late:
+        send(0, 0, c, ("m", "p")[c % 2])
+    for c in late:
+        send(0, 0, c, "pair")
+    for c in early + late:
+        share(0, 0, c)
+    yield
+    relay(0, early + late)
+    yield
+    for c in early:
+        take(0, 1, c)
+        send(0, 1, c, "p")
+        send(0, 1, c, "m")
+        share(0, 1, c)
+    yield
+    rest(0, late + early)
+    yield
+    for c in late:
+        take(2, 0, c)
+        send(2, 0, c, "pair")
+        share(2, 0, c)
+    relay(1, early)
+    yield
+    for c in early:
+        take(2, 0, c)
+        share(2, 0, c)
+    for c in late:
+        take(0, 1, c)
+        share(0, 1, c)
+    yield
+    rest(1, early)
+    for c in late:
+        for ring in (1, 3, 2):
+            take(ring, 1, c)
+            share(ring, 1, c)
+    for c in early:
+        take(2, 1, c)
+        share(2, 1, c)
     yield
     if has_sib:
         for ring in (0, 1, 3, 2):
             for pair in (0, 1):
-                for half in (0, 1):
-                    take(ring, pair, half, 1)
+                for c in range(4):
+                    take(ring, pair, c, 1)
 
 
 def add_rows(rows, step, body):
@@ -206,64 +227,104 @@
 
 def scatter_shapes(rows, width):
     return [
-        pltpu.VMEM((2, rows // 2, width), BF16),
-        pltpu.VMEM((2, rows // 2, width), BF16),
         pltpu.VMEM((2, rows, width), BF16),
         pltpu.VMEM((2, rows, width), BF16),
-        pltpu.VMEM((rows, width), BF16),
+        pltpu.VMEM((2, rows, width), BF16),
+        pltpu.VMEM((2, rows, width), BF16),
+        pltpu.VMEM((4, rows, width), BF16),
     ]
 
 
-def scatter(wire, group, terms, bufs, tag, prepare):
+def scatter(wire, group, terms, bufs, tag, prepare, parts):
     relay_m, relay_p, from_m, from_p, from_pair = bufs
-    rows = terms.shape[1]
-    half_rows = rows // 2
-    cut = (pl.ds(0, half_rows), pl.ds(half_rows, half_rows))
-    step = 128
-
-    def part(ring, pair, half):
-        return terms.at[group.slot(ring, pair), cut[half]]
+    unit = terms.shape[1] // 8
+    cut = [pl.ds(start * unit, size * unit) for start, size, _ in parts]
+    late = [c for c in range(4) if parts[c][2]]
+    early = [c for c in range(4) if not parts[c][2]]
+    start = parts[late[0]][0]
+    first = pl.ds(start * unit, sum(parts[c][1] for c in late) * unit)
+    to_p, to_m, to_pair = group.peers["p"], group.peers["m"], group.peers["pair"]
+
+    def at(ring, pair, rows):
+        return terms.at[group.slot(ring, pair), rows]
 
     def add(target, *others):
-        def body(at):
-            total = target[at].astype(F32)
+        def body(rows):
+            total = target[rows].astype(F32)
             for other in others:
-                total = total + other[at].astype(F32)
-            target[at] = total.astype(BF16)
-
-        add_rows(half_rows, step, body)
-
-    for q in (1, 0):
-        prepare(2, q)
-        wire.push((tag, "rm", q), part(2, q, 0), relay_m.at[q], group.peers["p"])
-        wire.push((tag, "rp", q), part(2, q, 1), relay_p.at[q], group.peers["m"])
-    yield
-    for q in (1, 0):
-        prepare(1, q)
-        prepare(3, q)
-        wire.push((tag, "m", q, 1), part(1, q, 1), from_m.at[q, cut[1]], group.peers["p"])
-        wire.push((tag, "p", q, 0), part(3, q, 0), from_p.at[q, cut[0]], group.peers["m"])
-        yield
-        wire.take((tag, "rm", q), relay_m.at[q], group.peers["p"])
-        add(part(1, q, 0), relay_m.at[q])
-        wire.push((tag, "m", q, 0), part(1, q, 0), from_m.at[q, cut[0]], group.peers["p"])
-        wire.take((tag, "rp", q), relay_p.at[q], group.peers["p"])
-        add(part(3, q, 1), relay_p.at[q])
-        wire.push((tag, "p", q, 1), part(3, q, 1), from_p.at[q, cut[1]], group.peers["m"])
+                total = total + other[rows].astype(F32)
+            target[rows] = total.astype(BF16)
+
+        add_rows(target.shape[0], unit, body)
+
+    def cross(ring):
+        dst = from_pair.at[ring, first]
+        wire.push((tag, "first", ring), at(ring, 1, first), dst, to_pair)
+
+    def crossed(ring):
+        src = from_pair.at[ring, first]
+        wire.take((tag, "first", ring), src, to_pair)
+        add(at(ring, 0, first), src)
+
+    def far(q, which):
+        for c in which:
+            dst, to = ((relay_m, to_p), (relay_p, to_m))[c % 2]
+            wire.push((tag, "far", q, c), at(2, q, cut[c]), dst.at[q, cut[c]], to)
+
+    def single(q, which):
+        for c in which:
+            ring, dst, to = ((3, from_p, to_m), (1, from_m, to_p))[c % 2]
+            wire.push((tag, "one", q, c), at(ring, q, cut[c]), dst.at[q, cut[c]], to)
+
+    def double(q, which):
+        for c in which:
+            ring, via, dst, to = ((1, relay_m, from_m, to_p), (3, relay_p, from_p, to_m))[c % 2]
+            wire.take((tag, "far", q, c), via.at[q, cut[c]], to)
+            add(at(ring, q, cut[c]), via.at[q, cut[c]])
+            wire.push((tag, "two", q, c), at(ring, q, cut[c]), dst.at[q, cut[c]], to)
+
+    def arrive(q, which):
+        for c in which:
+            one, two = ((from_p, from_m), (from_m, from_p))[c % 2]
+            wire.take((tag, "one", q, c), one.at[q, cut[c]], to_p)
+            wire.take((tag, "two", q, c), two.at[q, cut[c]], to_p)
+
+    prepare(2, 1)
+    cross(2)
+    far(1, early)
+    prepare(2, 0)
+    far(0, early)
+    yield
+    prepare(1, 1)
+    cross(1)
+    prepare(3, 1)
+    cross(3)
+    single(1, early)
+    crossed(2)
+    far(0, late)
+    yield
+    double(1, early)
+    prepare(1, 0)
+    prepare(3, 0)
+    single(0, early)
+    yield
+    crossed(1)
+    crossed(3)
+    single(0, late)
+    double(0, early + late)
     yield
     prepare(0, 1)
-    for half in (0, 1):
-        wire.take((tag, "m", 1, half), from_m.at[1, cut[half]], group.peers["p"])
-        wire.take((tag, "p", 1, half), from_p.at[1, cut[half]], group.peers["p"])
-        add(part(0, 1, half), from_m.at[1, cut[half]], from_p.at[1, cut[half]])
-        wire.push((tag, "z", half), part(0, 1, half), from_pair.at[cut[half]], group.peers["pair"])
+    cross(0)
+    for c in early:
+        arrive(1, [c])
+        add(at(0, 1, cut[c]), from_m.at[1, cut[c]], from_p.at[1, cut[c]])
+        wire.push((tag, "last", c), at(0, 1, cut[c]), from_pair.at[0, cut[c]], to_pair)
     yield
     prepare(0, 0)
-    for half in (0, 1):
-        wire.take((tag, "m", 0, half), from_m.at[0, cut[half]], group.peers["p"])
-        wire.take((tag, "p", 0, half), from_p.at[0, cut[half]], group.peers["p"])
-    for half in (0, 1):
-        wire.take((tag, "z", half), from_pair.at[cut[half]], group.peers["p"])
+    arrive(0, early + late)
+    wire.take((tag, "first", 0), from_pair.at[0, first], to_pair)
+    for c in early:
+        wire.take((tag, "last", c), from_pair.at[0, cut[c]], to_pair)
 
 
 def total_shapes(width):
@@ -425,8 +486,8 @@
 
         lax.fori_loop(0, 4, one, 0)
 
-    gather0 = gather(wire, across, near0, "n0", 8)
-    gather1 = gather(wire, across, near1, "n1", 8)
+    gather0 = gather(wire, across, near0, "n0", QUARTER, 8)
+    gather1 = gather(wire, across, near1, "n1", QUARTER, 8)
     for step in range(5):
         next(gather0)
         for at in ORDER[2 * step : 2 * step + 2]:
@@ -438,7 +499,7 @@
         product(0, ring, pair)
         next(gather1, None)
 
-    scatter0 = scatter(wire, along, terms0, bufs0, "s0", prepare0)
+    scatter0 = scatter(wire, along, terms0, bufs0, "s0", prepare0, QUARTER)
     for _ in range(4):
         next(scatter0)
     run(gather1)
@@ -448,7 +509,9 @@
     ]
     for copy in leaving:
         copy.start()
-    scatter1 = scatter(wire, along, terms1, bufs1, "s1", lambda *at: product(1, *at))
+    scatter1 = scatter(
+        wire, along, terms1, bufs1, "s1", lambda *at: product(1, *at), QUARTER
+    )
     for _ in scatter1:
         next(scatter0, None)
     run(scatter0)
@@ -464,7 +527,7 @@
                     terms[h][own, at].astype(F32)
                     + bufs[2][0, at].astype(F32)
                     + bufs[3][0, at].astype(F32)
-                    + bufs[4][at].astype(F32)
+                    + bufs[4][0, at].astype(F32)
                 ).astype(BF16)
                 for h, bufs in ((0, bufs0), (1, bufs1))
             ],
@@ -506,15 +569,15 @@
         return carry
 
     lax.fori_loop(0, rows // 256, chunk, 0)
-    steps = gather(wire, along, grads, "g")
+    steps = gather(wire, along, grads, "g", MORE)
     next(steps)
     weights[:width] = dot(nodes[...], gpre_s[...], ((0,), (0,)))
     weights[width : 2 * width] = dot(msg_s[...], gpre_s[...], ((0,), (0,)))
     weights[2 * width : 3 * width] = dot(act_s[...], gproj_s[...], ((0,), (0,)))
     sums = total(wire, place, weights, sum_bufs, "w")
-    next(sums)
-    for _ in steps:
-        next(sums, None)
+    for following in (sums, steps, sums, steps, sums, steps, steps, steps, sums, sums):
+        next(following)
+    run(steps)
     run(sums)
     result = sum_bufs[0]
     factor = F32(131072.0) ** F32(-0.5)
@@ -553,8 +616,8 @@
         + [pltpu.VMEM((TOTAL_ROWS, width), F32)]
         + total_shapes(width)
         + [
-            pltpu.SemaphoreType.DMA((140,)),
-            pltpu.SemaphoreType.DMA((140,)),
+            pltpu.SemaphoreType.DMA((240,)),
+            pltpu.SemaphoreType.DMA((240,)),
             pltpu.SemaphoreType.DMA((12,)),
         ],
         compiler_params=remote_params(2),
@@ -709,7 +772,7 @@
         add_rows(rows, 128, body)
 
     bufs = (relay_m, relay_p, from_m, from_p, from_pair)
-    run(scatter(wire, group, terms, bufs, "b", prepare))
+    run(scatter(wire, group, terms, bufs, "b", prepare, MORE))
     own = group.slot(0, 0)
 
     def last(at):
@@ -718,7 +781,7 @@
             + terms[own, at].astype(F32)
             + from_m[0, at].astype(F32)
             + from_p[0, at].astype(F32)
-            + from_pair[at].astype(F32)
+            + from_pair[0, at].astype(F32)
         ).astype(BF16)
 
     add_rows(rows, 128, last)

time: 206 us -> 192 us (0.932)
  Pallas kernels: 200 us -> 186 us
    pallas_call x1, Pallas kernels: 131 us -> 124 us  [middle(): pl.pallas_call(middle_kernel, out_shape=[near, near, jax.ShapeDtypeStruct...]
    pallas_call x1, Pallas kernels: 43.2 us -> 38.1 us  [finish(): pl.pallas_call(finish_kernel, out_shape=jax.ShapeDtypeStruct((rows, width...]
where the time goes in v5:
time: 192 us
  Pallas kernels  186 us (97%)
  local copies, waits for them, and re-layouts  2.64 us (1%)
  other arithmetic  2.07 us (1%)
    pallas_call x1, Pallas kernels, middle(): pl.pallas_call(middle_kernel, out_shape=[near, near, jax.ShapeDtypeStruct...  124 us
    pallas_call x1, Pallas kernels, finish(): pl.pallas_call(finish_kernel, out_shape=jax.ShapeDtypeStruct((rows, width...  38.1 us
    pallas_call x1, Pallas kernels, backward(): pl.pallas_call(backward_kernel, out_shape=[jax.ShapeDtypeStruct(tiles.sha...  24.2 us

profile of v5, /device:TPU:1, one launch (start us, length us, event | category | flops | bytes accessed | tf_op | source)
XLA Modules:
  0.0 191.8 jit_solution(4806656194775050409)
XLA Ops:
  0.6 0.8 copy.16
  1.4 0.6 clamp_bitcast_fusion.cols
  2.0 1.4 fusion.live
  3.5 124.1 %middle.1 = (bf16[128,128,128]{2,1,0:T(8,128)(2,1)}, bf16[128,128,128]{2,1,0:T(8,128)(2,1)}, bf16[8,1024,256]{2,1,0:T(8,128)(2,1)}, bf16[1024,256]{1,0:T(8,128)(...) custom-call(s32[64,4]{1,0:T(8,128)} %clamp_bitcast_fusion.cols, ...), custom_call_target="tpu_custom_call" | custom-call | tf_op jit(solution)/shard_map/middle/pallas_call | solution.py:597
  127.6 24.2 %backward.1 = (bf16[64,4,128,128]{3,2,1,0:T(8,128)(2,1)}, bf16[128,128,256]{2,1,0:T(8,128)(2,1)}, bf16[1024,256]{1,0:T(8,128)(2,1)}, f32[512,256]{1,0:T(8,128)}, f32[256,256]{1,0:T(8,128)}, /*index=5*/f32[3,256]{1,0:T(4,128)}) custom-call(s32[64,4]{1,0:T(8,128)} %clamp_bitcast_fusion.cols, s32[64]{0:T(128)} %bitcast.19, bf16[64,4,128,128]{3,2,1,0:T(8,128)(2,1)} %bitcast.14, ...), custom_call_target="tpu_custom_call" | custom-call | tf_op jit(solution)/shard_map/backward/pallas_call | solution.py:711
  151.8 38.1 %finish.1 = bf16[1024,256]{1,0:T(8,128)(2,1)} custom-call(bf16[16,1024,256]{2,1,0:T(8,128)(2,1)} %bitcast.15, f32[1024,256]{1,0:T(8,128)} %get-tuple-element.29.direct), custom_call_target="tpu_custom_call" | custom-call | tf_op jit(solution)/shard_map/finish/pallas_call | solution.py:793
  189.9 1.9 copy.19

commit v6 on v5

--- a/solution.py
+++ b/solution.py
@@ -132,6 +132,9 @@
             return buf.at[slot, pl.ds(start * unit, size * unit)]
         return buf.at[pl.ds(slot * per + start, size)]
 
+    def whole(slot):
+        return buf.at[slot] if per == 1 else buf.at[pl.ds(slot * per, per)]
+
     has_sib = "sib" in group.peers
     late = [c for c in range(4) if parts[c][2]]
     early = [c for c in range(4) if not parts[c][2]]
@@ -142,13 +145,14 @@
         name = (tag, (ring + dr) % 4, (pair + dp) % 2, dk, part)
         wire.push(name, ref, ref, group.peers[way])
 
-    def take(ring, pair, part, sib=0):
-        slot = group.slot(ring, pair, 1) if sib else group.slot(ring, pair)
-        wire.take((tag, ring, pair, sib, part), view(slot, part), group.peers["p"])
-
-    def share(ring, pair, part):
+    def take(ring, pair, part):
+        slot = group.slot(ring, pair)
+        wire.take((tag, ring, pair, 0, part), view(slot, part), group.peers["p"])
+
+    def share(ring, pair):
         if has_sib:
-            send(ring, pair, part, "sib")
+            ref = whole(group.slot(ring, pair))
+            wire.push((tag, ring, pair, 1), ref, ref, group.peers["sib"])
 
     def relay(pair, which):
         for c in which:
@@ -157,7 +161,6 @@
             send(ring, pair, c, way)
             if c in late and pair == 0:
                 send(ring, pair, c, "pair")
-            share(ring, pair, c)
 
     def rest(pair, which):
         for c in which:
@@ -165,7 +168,6 @@
             take(ring, pair, c)
             if c in late and pair == 0:
                 send(ring, pair, c, "pair")
-            share(ring, pair, c)
 
     for c in early:
         send(0, 0, c, "pair")
@@ -175,8 +177,7 @@
         send(0, 0, c, ("m", "p")[c % 2])
     for c in late:
         send(0, 0, c, "pair")
-    for c in early + late:
-        share(0, 0, c)
+    share(0, 0)
     yield
     relay(0, early + late)
     yield
@@ -184,37 +185,37 @@
         take(0, 1, c)
         send(0, 1, c, "p")
         send(0, 1, c, "m")
-        share(0, 1, c)
     yield
     rest(0, late + early)
+    share(1, 0)
+    share(3, 0)
     yield
     for c in late:
         take(2, 0, c)
         send(2, 0, c, "pair")
-        share(2, 0, c)
     relay(1, early)
     yield
     for c in early:
         take(2, 0, c)
-        share(2, 0, c)
+    share(2, 0)
     for c in late:
         take(0, 1, c)
-        share(0, 1, c)
+    share(0, 1)
     yield
     rest(1, early)
-    for c in late:
-        for ring in (1, 3, 2):
+    for ring in (1, 3):
+        for c in late:
             take(ring, 1, c)
-            share(ring, 1, c)
-    for c in early:
+        share(ring, 1)
+    for c in early + late:
         take(2, 1, c)
-        share(2, 1, c)
+    share(2, 1)
     yield
     if has_sib:
-        for ring in (0, 1, 3, 2):
-            for pair in (0, 1):
-                for c in range(4):
-                    take(ring, pair, c, 1)
+        for pair in (0, 1):
+            for ring in (0, 1, 3, 2):
+                slot = group.slot(ring, pair, 1)
+                wire.take((tag, ring, pair, 1), whole(slot), group.peers["p"])
 
 
 def add_rows(rows, step, body):
@@ -327,77 +328,79 @@
         wire.take((tag, "last", c), from_pair.at[0, cut[c]], to_pair)
 
 
-def total_shapes(width):
-    return [
-        pltpu.VMEM((TOTAL_ROWS, width), F32),
-        pltpu.VMEM((TOTAL_ROWS // 2, width), F32),
-        pltpu.VMEM((3, TOTAL_ROWS // 8, width), F32),
-        pltpu.VMEM((3, TOTAL_ROWS // 32, width), F32),
-        pltpu.VMEM((4, TOTAL_ROWS // 32, width), F32),
-    ]
-
-
-def total(wire, place, mine, bufs, tag):
-    result, in_core, in_x, in_y, in_z = bufs
-    half, quarter, piece = TOTAL_ROWS // 2, TOTAL_ROWS // 8, TOTAL_ROWS // 32
-
-    def span(core, x=None, y=None):
-        start, size = core * half, half
-        if x is not None:
-            start, size = start + x * quarter, quarter
-        if y is not None:
-            start, size = start + y * piece, piece
-        return pl.ds(pl.multiple_of(start, piece), size)
-
-    core, x, y = place.core, place.x, place.y
-    z = place.zh * 2 + place.zl
-    other = 1 - core
+def exchange(wire, tag, axis, place, part, dst):
+    for d in (1, 2, 3):
+        wire.push((tag, axis, d), part(d), dst(d), place.peer(**{axis: d}))
+
+
+def block(index, rows):
+    return pl.ds(pl.multiple_of(index * rows, rows), rows)
+
+
+def total_near(wire, place, mine, result, in_core, in_x, tag):
+    half, quarter = TOTAL_ROWS // 2, TOTAL_ROWS // 8
+    core, x = place.core, place.x
     sib = place.peer(core=1)
-    wire.push((tag, "core"), mine.at[span(other)], in_core, sib)
+    wire.push((tag, "core"), mine.at[block(1 - core, half)], in_core, sib)
     yield
     wire.take((tag, "core"), in_core, sib)
 
     def fold(i, carry):
         at = pl.ds(pl.multiple_of(core * half + i * 64, 64), 64)
-        mine[at] += in_core[pl.ds(pl.multiple_of(i * 64, 64), 64)]
+        mine[at] += in_core[block(i, 64)]
         return carry
 
     lax.fori_loop(0, half // 64, fold, 0)
-    for d in (1, 2, 3):
-        to = place.peer(x=d)
-        wire.push((tag, "x", d), mine.at[span(core, lax.rem(x + d, 4))], in_x.at[d - 1], to)
+
+    def own(index):
+        return mine.at[block(core * 4 + index, quarter)]
+
+    exchange(
+        wire, tag, "x", place, lambda d: own(lax.rem(x + d, 4)), lambda d: in_x.at[d - 1]
+    )
     yield
     for d in (1, 2, 3):
         wire.take((tag, "x", d), in_x.at[d - 1], sib)
-    mine[span(core, x)] += in_x[0] + in_x[1] + in_x[2]
+    at = block(x, quarter)
+    result[at] = mine[block(core * 4 + x, quarter)] + in_x[0] + in_x[1] + in_x[2]
+    exchange(wire, tag + "r", "x", place, lambda d: result.at[at], lambda d: result.at[at])
+    yield
     for d in (1, 2, 3):
-        to = place.peer(y=d)
-        wire.push((tag, "y", d), mine.at[span(core, x, lax.rem(y + d, 4))], in_y.at[d - 1], to)
+        wire.take((tag + "r", "x", d), result.at[block(lax.rem(x + 4 - d, 4), quarter)], sib)
+
+
+def total_far(wire, place, mine, result, in_y, in_z, tag):
+    quarter = TOTAL_ROWS // 8
+    core, y = place.core, place.y
+    z = place.zh * 2 + place.zl
+    sib = place.peer(core=1)
+    exchange(
+        wire,
+        tag,
+        "y",
+        place,
+        lambda d: mine.at[block(lax.rem(y + d, 4), quarter)],
+        lambda d: in_y.at[d - 1],
+    )
     yield
     for d in (1, 2, 3):
         wire.take((tag, "y", d), in_y.at[d - 1], sib)
-    in_z[z] = mine[span(core, x, y)] + in_y[0] + in_y[1] + in_y[2]
-    for d in (1, 2, 3):
-        wire.push((tag, "z", d), in_z.at[z], in_z.at[z], place.peer(z=d))
+    in_z[z] = mine[block(y, quarter)] + in_y[0] + in_y[1] + in_y[2]
+    exchange(wire, tag, "z", place, lambda d: in_z.at[z], lambda d: in_z.at[z])
     yield
     for d in (1, 2, 3):
         wire.take((tag, "z", d), in_z.at[lax.rem(z + 4 - d, 4)], sib)
-    at = span(core, x, y)
+    at = block(core * 4 + y, quarter)
     result[at] = in_z[0] + in_z[1] + in_z[2] + in_z[3]
+    exchange(wire, tag + "r", "y", place, lambda d: result.at[at], lambda d: result.at[at])
+    yield
     for d in (1, 2, 3):
-        wire.push((tag, "back y", d), result.at[at], result.at[at], place.peer(y=d))
-    yield
-    for d in (1, 2, 3):
-        wire.take((tag, "back y", d), result.at[span(core, x, lax.rem(y + 4 - d, 4))], sib)
-    at = span(core, x)
-    for d in (1, 2, 3):
-        wire.push((tag, "back x", d), result.at[at], result.at[at], place.peer(x=d))
-    yield
-    for d in (1, 2, 3):
-        wire.take((tag, "back x", d), result.at[span(core, lax.rem(x + 4 - d, 4))], sib)
-    wire.push((tag, "back core"), result.at[span(core)], result.at[span(core)], sib)
-    yield
-    wire.take((tag, "back core"), result.at[span(other)], sib)
+        there = block(core * 4 + lax.rem(y + 4 - d, 4), quarter)
+        wire.take((tag + "r", "y", d), result.at[there], sib)
+    half = block(core, TOTAL_ROWS // 2)
+    wire.push((tag, "join"), result.at[half], result.at[half], sib)
+    yield
+    wire.take((tag, "join"), result.at[block(1 - core, TOTAL_ROWS // 2)], sib)
 
 
 def run(steps):
@@ -424,12 +427,11 @@
 
 def middle_kernel(
     cols, live, tiles, nodes_any, nodes, cot, w_in, bias, w_out, gain, shift,
-    near0_out, near1_out, grads, updated, direct, gw_in, gw_out, gvec,
+    near0_out, near1_out, grads, updated, direct, part_sum,
     near0, near1, slots, terms0, terms1, *rest,
 ):
     bufs0, bufs1, rest = rest[:5], rest[5:10], rest[10:]
-    msg_s, act_s, gproj_s, gpre_s, weights = rest[:5]
-    sum_bufs, (send, recv, load) = rest[5:10], rest[10:]
+    msg_s, act_s, gproj_s, gpre_s, weights, in_core, in_x, send, recv, load = rest
     place = Place()
     across, along = RowGroup(place), ColGroup(place)
     width = nodes.shape[1]
@@ -574,16 +576,11 @@
     weights[:width] = dot(nodes[...], gpre_s[...], ((0,), (0,)))
     weights[width : 2 * width] = dot(msg_s[...], gpre_s[...], ((0,), (0,)))
     weights[2 * width : 3 * width] = dot(act_s[...], gproj_s[...], ((0,), (0,)))
-    sums = total(wire, place, weights, sum_bufs, "w")
-    for following in (sums, steps, sums, steps, sums, steps, steps, steps, sums, sums):
+    sums = total_near(wire, place, weights, part_sum, in_core, in_x, "w")
+    for following in (sums, steps, sums, steps, steps, sums, steps, steps):
         next(following)
     run(steps)
     run(sums)
-    result = sum_bufs[0]
-    factor = F32(131072.0) ** F32(-0.5)
-    gw_in[...] = result[: 2 * width] * factor
-    gw_out[...] = result[2 * width : 3 * width] * factor
-    gvec[...] = result[3 * width : 3 * width + 3] * factor
     for copy in leaving:
         copy.wait()
     wire.drain()
@@ -602,19 +599,20 @@
             jax.ShapeDtypeStruct((8, rows, width), BF16),
             jax.ShapeDtypeStruct((rows, width), BF16),
             jax.ShapeDtypeStruct((rows, width), F32),
-            jax.ShapeDtypeStruct((2 * width, width), F32),
-            jax.ShapeDtypeStruct((width, width), F32),
-            jax.ShapeDtypeStruct((3, width), F32),
+            jax.ShapeDtypeStruct((TOTAL_ROWS // 2, width), F32),
         ],
         in_specs=[smem, VM, ANY, ANY] + [VM] * 7,
-        out_specs=[ANY] * 2 + [VM] * 6,
+        out_specs=[ANY] * 2 + [VM] * 4,
         scratch_shapes=[pltpu.VMEM((128, 128, 128), BF16)] * 2
         + [pltpu.VMEM(tiles.shape, BF16)]
         + [pltpu.VMEM((8, rows, 128), BF16)] * 2
         + scatter_shapes(rows, 128) * 2
         + [one(BF16)] * 4
-        + [pltpu.VMEM((TOTAL_ROWS, width), F32)]
-        + total_shapes(width)
+        + [
+            pltpu.VMEM((TOTAL_ROWS, width), F32),
+            pltpu.VMEM((TOTAL_ROWS // 2, width), F32),
+            pltpu.VMEM((3, TOTAL_ROWS // 8, width), F32),
+        ]
         + [
             pltpu.SemaphoreType.DMA((240,)),
             pltpu.SemaphoreType.DMA((240,)),
@@ -626,15 +624,11 @@
 
 
 def backward_kernel(
-    cols, count, tiles, near0, near1, grads, updated_in, gw_in_in, gw_out_in, gvec_in,
-    tile_grads, back, updated, gw_in, gw_out, gvec, acc,
+    cols, count, tiles, near0, near1, grads, updated_in, tile_grads, back, updated, acc
 ):
     step = pl.program_id(0)
     per = tiles.shape[0]
     updated[...] = updated_in[...]
-    gw_in[...] = gw_in_in[...]
-    gw_out[...] = gw_out_in[...]
-    gvec[...] = gvec_in[...]
 
     @pl.when(step == 0)
     def _():
@@ -696,7 +690,7 @@
         lax.fori_loop(0, acc.shape[0], put, 0)
 
 
-def backward(cols, count, tiles, near0, near1, grads, updated, gw_in, gw_out, gvec):
+def backward(cols, count, tiles, near0, near1, grads, updated):
     row_blocks = tiles.shape[0]
     width = grads.shape[1]
     columns = (128, 128, width)
@@ -704,17 +698,14 @@
     per = 8
     steps = row_blocks // per
 
-    def cut(array):
-        return pl.BlockSpec((array.shape[0] // steps, width), lambda s, *_: (s, 0))
-
-    passed = [cut(updated), cut(gw_in), cut(gw_out), pl.BlockSpec((3, width), lambda s, *_: (0, 0))]
+    passed = [pl.BlockSpec((updated.shape[0] // steps, width), lambda s, *_: (s, 0))]
     return pl.pallas_call(
         backward_kernel,
         out_shape=[
             jax.ShapeDtypeStruct(tiles.shape, BF16),
             jax.ShapeDtypeStruct(columns, BF16),
-        ]
-        + [jax.ShapeDtypeStruct(a.shape, a.dtype) for a in (updated, gw_in, gw_out, gvec)],
+            jax.ShapeDtypeStruct(updated.shape, BF16),
+        ],
         grid_spec=pltpu.PrefetchScalarGridSpec(
             num_scalar_prefetch=2,
             grid=(steps,),
@@ -734,24 +725,30 @@
         ),
         compiler_params=pltpu.CompilerParams(vmem_limit_bytes=VMEM_LIMIT),
         name="backward",
-    )(cols, count, tiles, near0, near1, grads, updated, gw_in, gw_out, gvec)
+    )(cols, count, tiles, near0, near1, grads, updated)
 
 
 def finish_kernel(
-    back, direct, out,
-    terms, others, relay_m, relay_p, from_m, from_p, from_pair, send, recv, load,
+    back, direct, part_sum, out, result,
+    terms, others, relay_m, relay_p, from_m, from_p, from_pair, mine, in_y, in_z, send, recv, load,
 ):
-    group = RowGroup(Place())
+    place = Place()
+    group = RowGroup(place)
     rows = terms.shape[1]
 
     def loader(ring, pair):
         slot = group.slot(ring, pair)
         return pltpu.make_async_copy(back.at[slot], terms.at[slot], load.at[ring * 2 + pair])
 
+    held = pltpu.make_async_copy(part_sum, mine, load.at[8])
+    held.start()
     for at in ORDER:
         loader(*at).start()
-    greet(list(group.peers.values()))
+    greet(place.all_peers())
     wire = Wire(send, recv)
+    held.wait()
+    sums = total_far(wire, place, mine, result, in_y, in_z, "w")
+    next(sums)
     for ring, pair in ORDER:
         wire.push(
             ("f", ring, pair),
@@ -772,7 +769,9 @@
         add_rows(rows, 128, body)
 
     bufs = (relay_m, relay_p, from_m, from_p, from_pair)
-    run(scatter(wire, group, terms, bufs, "b", prepare, MORE))
+    for point, _ in enumerate(scatter(wire, group, terms, bufs, "b", prepare, MORE)):
+        if point in (0, 3, 4):
+            next(sums)
     own = group.slot(0, 0)
 
     def last(at):
@@ -785,29 +784,61 @@
         ).astype(BF16)
 
     add_rows(rows, 128, last)
+    run(sums)
     wire.drain()
 
 
-def finish(back, direct):
+def finish(back, direct, part_sum):
     rows, width = direct.shape
     return pl.pallas_call(
         finish_kernel,
-        out_shape=jax.ShapeDtypeStruct((rows, width), BF16),
-        in_specs=[ANY, VM],
-        out_specs=VM,
+        out_shape=[
+            jax.ShapeDtypeStruct((rows, width), BF16),
+            jax.ShapeDtypeStruct((TOTAL_ROWS, width), F32),
+        ],
+        in_specs=[ANY, VM, ANY],
+        out_specs=[VM] * 2,
         scratch_shapes=[
             pltpu.VMEM((16, rows, width), BF16),
             pltpu.VMEM((8, rows, width), BF16),
         ]
         + scatter_shapes(rows, width)
         + [
+            pltpu.VMEM((TOTAL_ROWS // 2, width), F32),
+            pltpu.VMEM((3, TOTAL_ROWS // 8, width), F32),
+            pltpu.VMEM((4, TOTAL_ROWS // 8, width), F32),
             pltpu.SemaphoreType.DMA((60,)),
             pltpu.SemaphoreType.DMA((60,)),
             pltpu.SemaphoreType.DMA((9,)),
         ],
         compiler_params=remote_params(3),
         name="finish",
-    )(back.reshape(16, rows, width), direct)
+    )(back.reshape(16, rows, width), direct, part_sum)
+
+
+def write_kernel(grad, sums, grad_nodes, gw_in, gw_out, gvec):
+    width = gw_out.shape[1]
+    factor = F32(131072.0) ** F32(-0.5)
+    grad_nodes[...] = grad[...]
+    gw_in[...] = sums[: 2 * width] * factor
+    gw_out[...] = sums[2 * width : 3 * width] * factor
+    gvec[...] = sums[3 * width : 3 * width + 3] * factor
+
+
+def write(grad, sums):
+    width = grad.shape[1]
+    return pl.pallas_call(
+        write_kernel,
+        out_shape=[
+            jax.ShapeDtypeStruct(grad.shape, BF16),
+            jax.ShapeDtypeStruct((2 * width, width), F32),
+            jax.ShapeDtypeStruct((width, width), F32),
+            jax.ShapeDtypeStruct((3, width), F32),
+        ],
+        in_specs=[VM] * 2,
+        out_specs=[VM] * 4,
+        name="write",
+    )(grad, sums)
 
 
 def body(nodes, tiles, tile_col, tile_count, w_in, bias_in, w_out, ln_gain, ln_shift, cotangent):
@@ -817,13 +848,12 @@
     cols = jnp.clip(cols, 0, 127)
     live = lax.broadcasted_iota(jnp.int32, (64, 4, 128), 1) < count[:, None, None]
     live = live.astype(F32)
-    near0, near1, grads, updated, direct, gw_in, gw_out, gvec = middle(
+    near0, near1, grads, updated, direct, part_sum = middle(
         cols, live, slots, nodes, cotangent, w_in, bias_in[None], w_out, ln_gain[None], ln_shift[None]
     )
-    grad_tiles, back, updated, gw_in, gw_out, gvec = backward(
-        cols, count, slots, near0, near1, grads.reshape(8 * rows, width), updated, gw_in, gw_out, gvec
-    )
-    grad_nodes = finish(back, direct)
+    grads = grads.reshape(8 * rows, width)
+    grad_tiles, back, updated = backward(cols, count, slots, near0, near1, grads, updated)
+    grad_nodes, gw_in, gw_out, gvec = write(*finish(back, direct, part_sum))
     return updated, grad_nodes, grad_tiles[:, None], gw_in, gw_out, gvec
 
 

time: 192 us -> 182 us (0.948)
  the two profiles are of different devices: /device:TPU:1 before, /device:TPU:24 now
where the time goes in v6:
time: 182 us; the launch traced here: 181 us
  Pallas kernels  178 us (98%)
  other arithmetic  2.07 us (1%)
    pallas_call x1, Pallas kernels, middle(): pl.pallas_call(middle_kernel, out_shape=[near, near, jax.ShapeDtypeStruct...  106 us
    pallas_call x1, Pallas kernels, finish(): pl.pallas_call(finish_kernel, out_shape=[jax.ShapeDtypeStruct((rows, widt...  44.1 us
    pallas_call x1, Pallas kernels, backward(): pl.pallas_call(backward_kernel, out_shape=[jax.ShapeDtypeStruct(tiles.sha...  25.4 us

profile of v6, /device:TPU:24, one launch (start us, length us, event | category | flops | bytes accessed | tf_op | source)
XLA Modules:
  0.0 181.2 jit_solution(3373460711704768862)
XLA Ops:
  0.6 0.8 copy.16
  1.4 0.6 clamp_bitcast_fusion.cols
  2.0 1.4 fusion.live
  3.5 105.7 %middle.1 = (bf16[128,128,128]{2,1,0:T(8,128)(2,1)}, bf16[128,128,128]{2,1,0:T(8,128)(2,1)}, bf16[8,1024,256]{2,1,0:T(8,128)(2,1)}, bf16[1024,256]{1,0:T(8,128)(...) custom-call(s32[64,4]{1,0:T(8,128)} %clamp_bitcast_fusion.cols, f32[64,4,128]{2,1,0:T(4,128)} %fusion.live, ...), custom_call_target="tpu_custom_call" | custom-call | tf_op jit(solution)/shard_map/middle/pallas_call | solution.py:594
  109.2 25.4 %backward.1 = (bf16[64,4,128,128]{3,2,1,0:T(8,128)(2,1)}, bf16[128,128,256]{2,1,0:T(8,128)(2,1)}, bf16[1024,256]{1,0:T(8,128)(2,1)}) custom-call(s32[64,4]{1,0:T(8,128)} %clamp_bitcast_fusion.cols, s32[64]{0:T(128)} %bitcast.19, bf16[64,4,128,128]{3,2,1,0:T(8,128)(2,1)} %bitcast.14, bf16[128,128,128]{2,1,0:T(8,128)(2,1)} %get-tuple-element.21.near0, ...), custom_call_target="tpu_custom_call" | custom-call | tf_op jit(solution)/shard_map/backward/pallas_call | solution.py:702
  134.6 44.1 %finish.1 = (bf16[1024,256]{1,0:T(8,128)(2,1)}, f32[1024,256]{1,0:T(8,128)}) custom-call(bf16[16,1024,256]{2,1,0:T(8,128)(2,1)} %bitcast.15, f32[1024,256]{1,0:T(8,128)} %get-tuple-element.27.direct, f32[512,256]{1,0:T(8,128)} %get-tuple-element.28.part_sum), custom_call_target="tpu_custom_call" | custom-call | tf_op jit(solution)/shard_map/finish/pallas_call | solution.py:793
  178.7 2.5 %write.1 = (bf16[1024,256]{1,0:T(8,128)(2,1)}, f32[512,256]{1,0:T(8,128)}, f32[256,256]{1,0:T(8,128)}, f32[3,256]{1,0:T(4,128)}) custom-call(bf16[1024,256]{1,0:T(8,128)(2,1)} %get-tuple-element.29.grad, f32[1024,256]{1,0:T(8,128)} %get-tuple-element.30.sums), custom_call_target="tpu_custom_call" | custom-call | tf_op jit(solution)/shard_map/write/pallas_call | solution.py:830

commit v7 on v6

--- a/solution.py
+++ b/solution.py
@@ -370,29 +370,38 @@
 
 
 def total_far(wire, place, mine, result, in_y, in_z, tag):
-    quarter = TOTAL_ROWS // 8
-    core, y = place.core, place.y
+    piece, quarter = TOTAL_ROWS // 32, TOTAL_ROWS // 8
+    core, x, y = place.core, place.x, place.y
     z = place.zh * 2 + place.zl
     sib = place.peer(core=1)
+
+    def at(x_at, y_at):
+        return block(core * 16 + y_at * 4 + x_at, piece)
+
     exchange(
         wire,
         tag,
         "y",
         place,
-        lambda d: mine.at[block(lax.rem(y + d, 4), quarter)],
+        lambda d: mine.at[block(lax.rem(y + d, 4) * 4 + x, piece)],
         lambda d: in_y.at[d - 1],
     )
     yield
     for d in (1, 2, 3):
         wire.take((tag, "y", d), in_y.at[d - 1], sib)
-    in_z[z] = mine[block(y, quarter)] + in_y[0] + in_y[1] + in_y[2]
+    in_z[z] = mine[block(y * 4 + x, piece)] + in_y[0] + in_y[1] + in_y[2]
     exchange(wire, tag, "z", place, lambda d: in_z.at[z], lambda d: in_z.at[z])
     yield
     for d in (1, 2, 3):
         wire.take((tag, "z", d), in_z.at[lax.rem(z + 4 - d, 4)], sib)
-    at = block(core * 4 + y, quarter)
-    result[at] = in_z[0] + in_z[1] + in_z[2] + in_z[3]
-    exchange(wire, tag + "r", "y", place, lambda d: result.at[at], lambda d: result.at[at])
+    result[at(x, y)] = in_z[0] + in_z[1] + in_z[2] + in_z[3]
+    own = result.at[at(x, y)]
+    exchange(wire, tag + "r", "x", place, lambda d: own, lambda d: own)
+    yield
+    for d in (1, 2, 3):
+        wire.take((tag + "r", "x", d), result.at[at(lax.rem(x + 4 - d, 4), y)], sib)
+    four = result.at[block(core * 4 + y, quarter)]
+    exchange(wire, tag + "r", "y", place, lambda d: four, lambda d: four)
     yield
     for d in (1, 2, 3):
         there = block(core * 4 + lax.rem(y + 4 - d, 4), quarter)
@@ -465,8 +474,9 @@
         base = along.slot(ring, pair) * 8
 
         def one(i, carry):
+            held = jnp.broadcast_to(live[pl.ds(base + i, 1)], (1, 128))
             for k in range(4):
-                keep = live[base + i, pl.ds(k, 1)].astype(BF16)
+                keep = (held > k).astype(F32).astype(BF16)
                 slots[base + i, k] = slots[base + i, k] * keep
             return carry
 
@@ -624,7 +634,9 @@
 
 
 def backward_kernel(
-    cols, count, tiles, near0, near1, grads, updated_in, tile_grads, back, updated, acc
+    cols, count, tiles, near0_any, near1_any, grads, updated_in,
+    tile_grads, back_any, updated,
+    acc, near0, near1, back, load, leave,
 ):
     step = pl.program_id(0)
     per = tiles.shape[0]
@@ -632,11 +644,20 @@
 
     @pl.when(step == 0)
     def _():
+        copies = [
+            pltpu.make_async_copy(near0_any, near0, load.at[0]),
+            pltpu.make_async_copy(near1_any, near1, load.at[1]),
+        ]
+        for copy in copies:
+            copy.start()
+
         def clear(i, carry):
             acc[i] = jnp.zeros(acc.shape[1:], F32)
             return carry
 
         lax.fori_loop(0, acc.shape[0], clear, 0)
+        for copy in copies:
+            copy.wait()
 
     scale = F32(256.0) ** F32(-0.5)
 
@@ -687,14 +708,20 @@
             back[i] = acc[i].astype(BF16)
             return carry
 
-        lax.fori_loop(0, acc.shape[0], put, 0)
+        copies = []
+        for part in range(8):
+            lax.fori_loop(part * 16, part * 16 + 16, put, 0)
+            at = pl.ds(part * 16, 16)
+            copies.append(pltpu.make_async_copy(back.at[at], back_any.at[at], leave.at[part]))
+            copies[-1].start()
+        for copy in copies:
+            copy.wait()
 
 
 def backward(cols, count, tiles, near0, near1, grads, updated):
     row_blocks = tiles.shape[0]
     width = grads.shape[1]
     columns = (128, 128, width)
-    near = pl.BlockSpec(near0.shape, lambda s, *_: (0, 0, 0), pipeline_mode=pl.Buffered(1))
     per = 8
     steps = row_blocks // per
 
@@ -711,17 +738,24 @@
             grid=(steps,),
             in_specs=[
                 pl.BlockSpec((per, 4, 128, 128), lambda s, *_: (s, 0, 0, 0)),
-                near,
-                near,
+                ANY,
+                ANY,
                 pl.BlockSpec((per * 128, width), lambda s, *_: (s, 0)),
             ]
             + passed,
             out_specs=[
                 pl.BlockSpec((per, 4, 128, 128), lambda s, *_: (s, 0, 0, 0)),
-                pl.BlockSpec(columns, lambda s, *_: (0, 0, 0), pipeline_mode=pl.Buffered(1)),
+                ANY,
             ]
             + passed,
-            scratch_shapes=[pltpu.VMEM(columns, F32)],
+            scratch_shapes=[
+                pltpu.VMEM(columns, F32),
+                pltpu.VMEM(near0.shape, BF16),
+                pltpu.VMEM(near1.shape, BF16),
+                pltpu.VMEM(columns, BF16),
+                pltpu.SemaphoreType.DMA((2,)),
+                pltpu.SemaphoreType.DMA((8,)),
+            ],
         ),
         compiler_params=pltpu.CompilerParams(vmem_limit_bytes=VMEM_LIMIT),
         name="backward",
@@ -770,7 +804,7 @@
 
     bufs = (relay_m, relay_p, from_m, from_p, from_pair)
     for point, _ in enumerate(scatter(wire, group, terms, bufs, "b", prepare, MORE)):
-        if point in (0, 3, 4):
+        if point in (0, 1, 3, 4):
             next(sums)
     own = group.slot(0, 0)
 
@@ -805,8 +839,8 @@
         + scatter_shapes(rows, width)
         + [
             pltpu.VMEM((TOTAL_ROWS // 2, width), F32),
-            pltpu.VMEM((3, TOTAL_ROWS // 8, width), F32),
-            pltpu.VMEM((4, TOTAL_ROWS // 8, width), F32),
+            pltpu.VMEM((3, TOTAL_ROWS // 32, width), F32),
+            pltpu.VMEM((4, TOTAL_ROWS // 32, width), F32),
             pltpu.SemaphoreType.DMA((60,)),
             pltpu.SemaphoreType.DMA((60,)),
             pltpu.SemaphoreType.DMA((9,)),
@@ -846,10 +880,8 @@
     cols, count = tile_col[:, 0], tile_count[:, 0]
     slots = tiles[:, 0]
     cols = jnp.clip(cols, 0, 127)
-    live = lax.broadcasted_iota(jnp.int32, (64, 4, 128), 1) < count[:, None, None]
-    live = live.astype(F32)
     near0, near1, grads, updated, direct, part_sum = middle(
-        cols, live, slots, nodes, cotangent, w_in, bias_in[None], w_out, ln_gain[None], ln_shift[None]
+        cols, tile_count, slots, nodes, cotangent, w_in, bias_in[None], w_out, ln_gain[None], ln_shift[None]
     )
     grads = grads.reshape(8 * rows, width)
     grad_tiles, back, updated = backward(cols, count, slots, near0, near1, grads, updated)

time: 182 us -> 179 us (0.984)
  the two profiles are of different devices: /device:TPU:24 before, /device:TPU:1 now
where the time goes in v7:
time: 179 us; the launch traced here: 178 us
  Pallas kernels  175 us (98%)
  local copies, waits for them, and re-layouts  2.13 us (1%)
    pallas_call x1, Pallas kernels, middle(): pl.pallas_call(middle_kernel, out_shape=[near, near, jax.ShapeDtypeStruct...  107 us
    pallas_call x1, Pallas kernels, finish(): pl.pallas_call(finish_kernel, out_shape=[jax.ShapeDtypeStruct((rows, widt...  41.9 us
    pallas_call x1, Pallas kernels, backward(): pl.pallas_call(backward_kernel, out_shape=[jax.ShapeDtypeStruct(tiles.sha...  23 us

profile of v7, /device:TPU:1, one launch (start us, length us, event | category | flops | bytes accessed | tf_op | source)
XLA Modules:
  0.0 178.2 jit_solution(2493134023849853139)
XLA Ops:
  0.6 0.8 copy.16
  1.4 0.6 clamp_bitcast_fusion.cols
  2.0 1.4 copy.17.live
  3.4 107.4 %middle.1 = (bf16[128,128,128]{2,1,0:T(8,128)(2,1)}, bf16[128,128,128]{2,1,0:T(8,128)(2,1)}, bf16[8,1024,256]{2,1,0:T(8,128)(2,1)}, bf16[1024,256]{1,0:T(8,128)(...) custom-call(s32[64,4]{1,0:T(8,128)} %clamp_bitcast_fusion.cols, s32[64,1]{1,0:T(8,128)} %copy.17.live, ...), custom_call_target="tpu_custom_call" | custom-call | tf_op jit(solution)/shard_map/middle/pallas_call | solution.py:604
  110.8 23.0 %backward.1 = (bf16[64,4,128,128]{3,2,1,0:T(8,128)(2,1)}, bf16[128,128,256]{2,1,0:T(8,128)(2,1)}, bf16[1024,256]{1,0:T(8,128)(2,1)}) custom-call(s32[64,4]{1,0:T(8,128)} %clamp_bitcast_fusion.cols, s32[64]{0:T(128)} %bitcast.18, bf16[64,4,128,128]{3,2,1,0:T(8,128)(2,1)} %bitcast.14, bf16[128,128,128]{2,1,0:T(8,128)(2,1)} %get-tuple-element.21.near0_any, ...), custom_call_target="tpu_custom_call" | custom-call | tf_op jit(solution)/shard_map/backward/pallas_call | solution.py:729
  133.8 41.9 %finish.1 = (bf16[1024,256]{1,0:T(8,128)(2,1)}, f32[1024,256]{1,0:T(8,128)}) custom-call(bf16[16,1024,256]{2,1,0:T(8,128)(2,1)} %bitcast.15, f32[1024,256]{1,0:T(8,128)} %get-tuple-element.27.direct, f32[512,256]{1,0:T(8,128)} %get-tuple-element.28.part_sum), custom_call_target="tpu_custom_call" | custom-call | tf_op jit(solution)/shard_map/finish/pallas_call | solution.py:827
  175.7 2.5 %write.1 = (bf16[1024,256]{1,0:T(8,128)(2,1)}, f32[512,256]{1,0:T(8,128)}, f32[256,256]{1,0:T(8,128)}, f32[3,256]{1,0:T(4,128)}) custom-call(bf16[1024,256]{1,0:T(8,128)(2,1)} %get-tuple-element.29.grad, f32[1024,256]{1,0:T(8,128)} %get-tuple-element.30.sums), custom_call_target="tpu_custom_call" | custom-call | tf_op jit(solution)/shard_map/write/pallas_call | solution.py:864

commit v8 on v7

--- a/solution.py
+++ b/solution.py
@@ -474,7 +474,7 @@
         base = along.slot(ring, pair) * 8
 
         def one(i, carry):
-            held = jnp.broadcast_to(live[pl.ds(base + i, 1)], (1, 128))
+            held = jnp.full((1, 128), live[base + i], jnp.int32)
             for k in range(4):
                 keep = (held > k).astype(F32).astype(BF16)
                 slots[base + i, k] = slots[base + i, k] * keep
@@ -498,12 +498,13 @@
 
         lax.fori_loop(0, 4, one, 0)
 
-    gather0 = gather(wire, across, near0, "n0", QUARTER, 8)
+    gather0 = gather(wire, across, near0, "n0", MORE, 8)
     gather1 = gather(wire, across, near1, "n1", QUARTER, 8)
-    for step in range(5):
+    next(gather0)
+    for at in ORDER:
+        mask(*at)
+    for _ in range(4):
         next(gather0)
-        for at in ORDER[2 * step : 2 * step + 2]:
-            mask(*at)
     next(gather1)
     run(gather0)
 
@@ -511,7 +512,7 @@
         product(0, ring, pair)
         next(gather1, None)
 
-    scatter0 = scatter(wire, along, terms0, bufs0, "s0", prepare0, QUARTER)
+    scatter0 = scatter(wire, along, terms0, bufs0, "s0", prepare0, MORE)
     for _ in range(4):
         next(scatter0)
     run(gather1)
@@ -522,7 +523,7 @@
     for copy in leaving:
         copy.start()
     scatter1 = scatter(
-        wire, along, terms1, bufs1, "s1", lambda *at: product(1, *at), QUARTER
+        wire, along, terms1, bufs1, "s1", lambda *at: product(1, *at), MORE
     )
     for _ in scatter1:
         next(scatter0, None)
@@ -611,7 +612,7 @@
             jax.ShapeDtypeStruct((rows, width), F32),
             jax.ShapeDtypeStruct((TOTAL_ROWS // 2, width), F32),
         ],
-        in_specs=[smem, VM, ANY, ANY] + [VM] * 7,
+        in_specs=[smem, smem, ANY, ANY] + [VM] * 7,
         out_specs=[ANY] * 2 + [VM] * 4,
         scratch_shapes=[pltpu.VMEM((128, 128, 128), BF16)] * 2
         + [pltpu.VMEM(tiles.shape, BF16)]
@@ -881,7 +882,7 @@
     slots = tiles[:, 0]
     cols = jnp.clip(cols, 0, 127)
     near0, near1, grads, updated, direct, part_sum = middle(
-        cols, tile_count, slots, nodes, cotangent, w_in, bias_in[None], w_out, ln_gain[None], ln_shift[None]
+        cols, count, slots, nodes, cotangent, w_in, bias_in[None], w_out, ln_gain[None], ln_shift[None]
     )
     grads = grads.reshape(8 * rows, width)
     grad_tiles, back, updated = backward(cols, count, slots, near0, near1, grads, updated)

time: 179 us -> 177 us (0.989)
    pallas_call x1, Pallas kernels: 107 us -> 105 us  [middle(): pl.pallas_call(middle_kernel, out_shape=[near, near, jax.ShapeDtypeStruct...]
where the time goes in v8:
time: 177 us; the launch traced here: 176 us
  Pallas kernels  174 us (98%)
    pallas_call x1, Pallas kernels, middle(): pl.pallas_call(middle_kernel, out_shape=[near, near, jax.ShapeDtypeStruct...  105 us
    pallas_call x1, Pallas kernels, finish(): pl.pallas_call(finish_kernel, out_shape=[jax.ShapeDtypeStruct((rows, widt...  42.4 us
    pallas_call x1, Pallas kernels, backward(): pl.pallas_call(backward_kernel, out_shape=[jax.ShapeDtypeStruct(tiles.sha...  24.3 us

profile of v8, /device:TPU:1, one launch (start us, length us, event | category | flops | bytes accessed | tf_op | source)
XLA Modules:
  0.0 175.8 jit_solution(14329155549303675554)
XLA Ops:
  0.6 0.8 copy.16
  1.4 0.6 clamp_bitcast_fusion.cols
  2.0 104.5 %middle.1 = (bf16[128,128,128]{2,1,0:T(8,128)(2,1)}, bf16[128,128,128]{2,1,0:T(8,128)(2,1)}, bf16[8,1024,256]{2,1,0:T(8,128)(2,1)}, bf16[1024,256]{1,0:T(8,128)(...) custom-call(s32[64,4]{1,0:T(8,128)} %clamp_bitcast_fusion.cols, s32[64]{0:T(128)} %bitcast.18, ...), custom_call_target="tpu_custom_call" | custom-call | tf_op jit(solution)/shard_map/middle/pallas_call | solution.py:605
  106.5 24.3 %backward.1 = (bf16[64,4,128,128]{3,2,1,0:T(8,128)(2,1)}, bf16[128,128,256]{2,1,0:T(8,128)(2,1)}, bf16[1024,256]{1,0:T(8,128)(2,1)}) custom-call(s32[64,4]{1,0:T(8,128)} %clamp_bitcast_fusion.cols, s32[64]{0:T(128)} %bitcast.19, bf16[64,4,128,128]{3,2,1,0:T(8,128)(2,1)} %bitcast.14, bf16[128,128,128]{2,1,0:T(8,128)(2,1)} %get-tuple-element.21.near0_any, ...), custom_call_target="tpu_custom_call" | custom-call | tf_op jit(solution)/shard_map/backward/pallas_call | solution.py:730
  130.9 42.4 %finish.1 = (bf16[1024,256]{1,0:T(8,128)(2,1)}, f32[1024,256]{1,0:T(8,128)}) custom-call(bf16[16,1024,256]{2,1,0:T(8,128)(2,1)} %bitcast.15, f32[1024,256]{1,0:T(8,128)} %get-tuple-element.27.direct, f32[512,256]{1,0:T(8,128)} %get-tuple-element.28.part_sum), custom_call_target="tpu_custom_call" | custom-call | tf_op jit(solution)/shard_map/finish/pallas_call | solution.py:828
  173.3 2.5 %write.1 = (bf16[1024,256]{1,0:T(8,128)(2,1)}, f32[512,256]{1,0:T(8,128)}, f32[256,256]{1,0:T(8,128)}, f32[3,256]{1,0:T(4,128)}) custom-call(bf16[1024,256]{1,0:T(8,128)(2,1)} %get-tuple-element.29.grad, f32[1024,256]{1,0:T(8,128)} %get-tuple-element.30.sums), custom_call_target="tpu_custom_call" | custom-call | tf_op jit(solution)/shard_map/write/pallas_call | solution.py:865

commit v9 on v8

--- a/solution.py
+++ b/solution.py
@@ -173,6 +173,7 @@
         send(0, 0, c, "pair")
     for c in early + late:
         send(0, 0, c, ("p", "m")[c % 2])
+    yield
     for c in early + late:
         send(0, 0, c, ("m", "p")[c % 2])
     for c in late:
@@ -501,10 +502,14 @@
     gather0 = gather(wire, across, near0, "n0", MORE, 8)
     gather1 = gather(wire, across, near1, "n1", QUARTER, 8)
     next(gather0)
-    for at in ORDER:
+    for at in ORDER[:4]:
+        mask(*at)
+    next(gather0)
+    for at in ORDER[4:]:
         mask(*at)
     for _ in range(4):
         next(gather0)
+    next(gather1)
     next(gather1)
     run(gather0)
 
@@ -585,6 +590,7 @@
     steps = gather(wire, along, grads, "g", MORE)
     next(steps)
     weights[:width] = dot(nodes[...], gpre_s[...], ((0,), (0,)))
+    next(steps)
     weights[width : 2 * width] = dot(msg_s[...], gpre_s[...], ((0,), (0,)))
     weights[2 * width : 3 * width] = dot(act_s[...], gproj_s[...], ((0,), (0,)))
     sums = total_near(wire, place, weights, part_sum, in_core, in_x, "w")
@@ -784,15 +790,23 @@
     held.wait()
     sums = total_far(wire, place, mine, result, in_y, in_z, "w")
     next(sums)
-    for ring, pair in ORDER:
-        wire.push(
-            ("f", ring, pair),
-            back.at[group.slot(ring, pair, 1)],
-            others.at[ring * 2 + pair],
-            group.peers["sib"],
-        )
+    ahead = iter(ORDER)
+
+    def swap():
+        for ring, pair in ahead:
+            wire.push(
+                ("f", ring, pair),
+                back.at[group.slot(ring, pair, 1)],
+                others.at[ring * 2 + pair],
+                group.peers["sib"],
+            )
+            return
+
+    swap()
+    swap()
 
     def prepare(ring, pair):
+        swap()
         loader(ring, pair).wait()
         other = others.at[ring * 2 + pair]
         wire.take(("f", ring, pair), other, group.peers["sib"])

time: 177 us -> 178 us (level)
    pallas_call x1, Pallas kernels: 42.4 us -> 44.2 us  [finish(): pl.pallas_call(finish_kernel, out_shape=[jax.ShapeDtypeStruct((rows, widt...]
where the time goes in v9:
time: 178 us; the launch traced here: 176 us
  Pallas kernels  174 us (98%)
    pallas_call x1, Pallas kernels, middle(): pl.pallas_call(middle_kernel, out_shape=[near, near, jax.ShapeDtypeStruct...  105 us
    pallas_call x1, Pallas kernels, finish(): pl.pallas_call(finish_kernel, out_shape=[jax.ShapeDtypeStruct((rows, widt...  44.2 us
    pallas_call x1, Pallas kernels, backward(): pl.pallas_call(backward_kernel, out_shape=[jax.ShapeDtypeStruct(tiles.sha...  23.2 us

profile of v9, /device:TPU:1, one launch (start us, length us, event | category | flops | bytes accessed | tf_op | source)
XLA Modules:
  0.0 176.4 jit_solution(11350001958450798920)
XLA Ops:
  0.6 0.8 copy.16
  1.4 0.6 clamp_bitcast_fusion.cols
  2.0 104.5 %middle.1 = (bf16[128,128,128]{2,1,0:T(8,128)(2,1)}, bf16[128,128,128]{2,1,0:T(8,128)(2,1)}, bf16[8,1024,256]{2,1,0:T(8,128)(2,1)}, bf16[1024,256]{1,0:T(8,128)(...) custom-call(s32[64,4]{1,0:T(8,128)} %clamp_bitcast_fusion.cols, s32[64]{0:T(128)} %bitcast.18, ...), custom_call_target="tpu_custom_call" | custom-call | tf_op jit(solution)/shard_map/middle/pallas_call | solution.py:611
  106.5 23.2 %backward.1 = (bf16[64,4,128,128]{3,2,1,0:T(8,128)(2,1)}, bf16[128,128,256]{2,1,0:T(8,128)(2,1)}, bf16[1024,256]{1,0:T(8,128)(2,1)}) custom-call(s32[64,4]{1,0:T(8,128)} %clamp_bitcast_fusion.cols, s32[64]{0:T(128)} %bitcast.19, bf16[64,4,128,128]{3,2,1,0:T(8,128)(2,1)} %bitcast.14, bf16[128,128,128]{2,1,0:T(8,128)(2,1)} %get-tuple-element.21.near0_any, ...), custom_call_target="tpu_custom_call" | custom-call | tf_op jit(solution)/shard_map/backward/pallas_call | solution.py:736
  129.7 44.2 %finish.1 = (bf16[1024,256]{1,0:T(8,128)(2,1)}, f32[1024,256]{1,0:T(8,128)}) custom-call(bf16[16,1024,256]{2,1,0:T(8,128)(2,1)} %bitcast.15, f32[1024,256]{1,0:T(8,128)} %get-tuple-element.27.direct, f32[512,256]{1,0:T(8,128)} %get-tuple-element.28.part_sum), custom_call_target="tpu_custom_call" | custom-call | tf_op jit(solution)/shard_map/finish/pallas_call | solution.py:842
  173.9 2.5 %write.1 = (bf16[1024,256]{1,0:T(8,128)(2,1)}, f32[512,256]{1,0:T(8,128)}, f32[256,256]{1,0:T(8,128)}, f32[3,256]{1,0:T(4,128)}) custom-call(bf16[1024,256]{1,0:T(8,128)(2,1)} %get-tuple-element.29.grad, f32[1024,256]{1,0:T(8,128)} %get-tuple-element.30.sums), custom_call_target="tpu_custom_call" | custom-call | tf_op jit(solution)/shard_map/write/pallas_call | solution.py:879

commit v10 on v9

--- a/solution.py
+++ b/solution.py
@@ -513,9 +513,12 @@
     next(gather1)
     run(gather0)
 
+    gather_steps = {(3, 1): 1, (1, 0): 2, (3, 0): 2}
+
     def prepare0(ring, pair):
         product(0, ring, pair)
-        next(gather1, None)
+        for _ in range(gather_steps.get((ring, pair), 0)):
+            next(gather1, None)
 
     scatter0 = scatter(wire, along, terms0, bufs0, "s0", prepare0, MORE)
     for _ in range(4):

time: 178 us -> 179 us (level)
  Pallas kernels: 174 us -> 176 us
    pallas_call x1, Pallas kernels: 105 us -> 107 us  [middle(): pl.pallas_call(middle_kernel, out_shape=[near, near, jax.ShapeDtypeStruct...]
    pallas_call x1, Pallas kernels: 44.2 us -> 42 us  [finish(): pl.pallas_call(finish_kernel, out_shape=[jax.ShapeDtypeStruct((rows, widt...]
where the time goes in v10:
time: 179 us; the launch traced here: 178 us
  Pallas kernels  176 us (98%)
    pallas_call x1, Pallas kernels, middle(): pl.pallas_call(middle_kernel, out_shape=[near, near, jax.ShapeDtypeStruct...  107 us
    pallas_call x1, Pallas kernels, finish(): pl.pallas_call(finish_kernel, out_shape=[jax.ShapeDtypeStruct((rows, widt...  42 us
    pallas_call x1, Pallas kernels, backward(): pl.pallas_call(backward_kernel, out_shape=[jax.ShapeDtypeStruct(tiles.sha...  24.5 us

profile of v10, /device:TPU:1, one launch (start us, length us, event | category | flops | bytes accessed | tf_op | source)
XLA Modules:
  0.0 178.2 jit_solution(13828452258843060328)
XLA Ops:
  0.6 0.8 copy.16
  1.4 0.6 clamp_bitcast_fusion.cols
  2.0 107.2 %middle.1 = (bf16[128,128,128]{2,1,0:T(8,128)(2,1)}, bf16[128,128,128]{2,1,0:T(8,128)(2,1)}, bf16[8,1024,256]{2,1,0:T(8,128)(2,1)}, bf16[1024,256]{1,0:T(8,128)(...) custom-call(s32[64,4]{1,0:T(8,128)} %clamp_bitcast_fusion.cols, s32[64]{0:T(128)} %bitcast.18, ...), custom_call_target="tpu_custom_call" | custom-call | tf_op jit(solution)/shard_map/middle/pallas_call | solution.py:614
  109.2 24.5 %backward.1 = (bf16[64,4,128,128]{3,2,1,0:T(8,128)(2,1)}, bf16[128,128,256]{2,1,0:T(8,128)(2,1)}, bf16[1024,256]{1,0:T(8,128)(2,1)}) custom-call(s32[64,4]{1,0:T(8,128)} %clamp_bitcast_fusion.cols, s32[64]{0:T(128)} %bitcast.19, bf16[64,4,128,128]{3,2,1,0:T(8,128)(2,1)} %bitcast.14, bf16[128,128,128]{2,1,0:T(8,128)(2,1)} %get-tuple-element.21.near0_any, ...), custom_call_target="tpu_custom_call" | custom-call | tf_op jit(solution)/shard_map/backward/pallas_call | solution.py:739
  133.7 42.0 %finish.1 = (bf16[1024,256]{1,0:T(8,128)(2,1)}, f32[1024,256]{1,0:T(8,128)}) custom-call(bf16[16,1024,256]{2,1,0:T(8,128)(2,1)} %bitcast.15, f32[1024,256]{1,0:T(8,128)} %get-tuple-element.27.direct, f32[512,256]{1,0:T(8,128)} %get-tuple-element.28.part_sum), custom_call_target="tpu_custom_call" | custom-call | tf_op jit(solution)/shard_map/finish/pallas_call | solution.py:845
  175.7 2.5 %write.1 = (bf16[1024,256]{1,0:T(8,128)(2,1)}, f32[512,256]{1,0:T(8,128)}, f32[256,256]{1,0:T(8,128)}, f32[3,256]{1,0:T(4,128)}) custom-call(bf16[1024,256]{1,0:T(8,128)(2,1)} %get-tuple-element.29.grad, f32[1024,256]{1,0:T(8,128)} %get-tuple-element.30.sums), custom_call_target="tpu_custom_call" | custom-call | tf_op jit(solution)/shard_map/write/pallas_call | solution.py:882

commit v11 on v9

--- a/solution.py
+++ b/solution.py
@@ -507,9 +507,10 @@
     next(gather0)
     for at in ORDER[4:]:
         mask(*at)
-    for _ in range(4):
+    for _ in range(3):
         next(gather0)
     next(gather1)
+    next(gather0)
     next(gather1)
     run(gather0)
 

time: 178 us -> 179 us (level)
  Pallas kernels: 174 us -> 176 us
    pallas_call x1, Pallas kernels: 105 us -> 107 us  [middle(): pl.pallas_call(middle_kernel, out_shape=[near, near, jax.ShapeDtypeStruct...]
where the time goes in v11:
time: 179 us; the launch traced here: 178 us
  Pallas kernels  176 us (98%)
    pallas_call x1, Pallas kernels, middle(): pl.pallas_call(middle_kernel, out_shape=[near, near, jax.ShapeDtypeStruct...  107 us
    pallas_call x1, Pallas kernels, finish(): pl.pallas_call(finish_kernel, out_shape=[jax.ShapeDtypeStruct((rows, widt...  42.7 us
    pallas_call x1, Pallas kernels, backward(): pl.pallas_call(backward_kernel, out_shape=[jax.ShapeDtypeStruct(tiles.sha...  23.2 us

profile of v11, /device:TPU:1, one launch (start us, length us, event | category | flops | bytes accessed | tf_op | source)
XLA Modules:
  0.0 177.9 jit_solution(7051495951425030039)
XLA Ops:
  0.6 0.8 copy.16
  1.4 0.6 clamp_bitcast_fusion.cols
  2.0 107.4 %middle.1 = (bf16[128,128,128]{2,1,0:T(8,128)(2,1)}, bf16[128,128,128]{2,1,0:T(8,128)(2,1)}, bf16[8,1024,256]{2,1,0:T(8,128)(2,1)}, bf16[1024,256]{1,0:T(8,128)(...) custom-call(s32[64,4]{1,0:T(8,128)} %clamp_bitcast_fusion.cols, s32[64]{0:T(128)} %bitcast.18, ...), custom_call_target="tpu_custom_call" | custom-call | tf_op jit(solution)/shard_map/middle/pallas_call | solution.py:612
  109.5 23.2 %backward.1 = (bf16[64,4,128,128]{3,2,1,0:T(8,128)(2,1)}, bf16[128,128,256]{2,1,0:T(8,128)(2,1)}, bf16[1024,256]{1,0:T(8,128)(2,1)}) custom-call(s32[64,4]{1,0:T(8,128)} %clamp_bitcast_fusion.cols, s32[64]{0:T(128)} %bitcast.19, bf16[64,4,128,128]{3,2,1,0:T(8,128)(2,1)} %bitcast.14, bf16[128,128,128]{2,1,0:T(8,128)(2,1)} %get-tuple-element.21.near0_any, ...), custom_call_target="tpu_custom_call" | custom-call | tf_op jit(solution)/shard_map/backward/pallas_call | solution.py:737
  132.7 42.7 %finish.1 = (bf16[1024,256]{1,0:T(8,128)(2,1)}, f32[1024,256]{1,0:T(8,128)}) custom-call(bf16[16,1024,256]{2,1,0:T(8,128)(2,1)} %bitcast.15, f32[1024,256]{1,0:T(8,128)} %get-tuple-element.27.direct, f32[512,256]{1,0:T(8,128)} %get-tuple-element.28.part_sum), custom_call_target="tpu_custom_call" | custom-call | tf_op jit(solution)/shard_map/finish/pallas_call | solution.py:843
  175.4 2.5 %write.1 = (bf16[1024,256]{1,0:T(8,128)(2,1)}, f32[512,256]{1,0:T(8,128)}, f32[256,256]{1,0:T(8,128)}, f32[3,256]{1,0:T(4,128)}) custom-call(bf16[1024,256]{1,0:T(8,128)(2,1)} %get-tuple-element.29.grad, f32[1024,256]{1,0:T(8,128)} %get-tuple-element.30.sums), custom_call_target="tpu_custom_call" | custom-call | tf_op jit(solution)/shard_map/write/pallas_call | solution.py:880
